TPU v7x, 512 devices: a whole 4x4x16 slice. The times are simulated.
512 devices in a mesh: inp: 16 (over z), tm: 8 (over y, x_hi), freq: 4 (over x_lo, core).
Axes of the slice: x: 4 (x_hi: 2, x_lo: 2; x = x_hi * 2 + x_lo), y: 4, z: 16, core: 2. Of those that a mesh axis runs over, the one named last changes fastest.
Arguments:
- volt: bfloat16 [2, 32768, 2048], P(None, 'tm', 'inp'), may hold values from -8 to 8
- window: float32 [4, 64], replicated, may hold values from 0.1 to 1
Outputs:
- spectra: bfloat16 [2, 512, 64, 2048], P(None, 'tm', ('freq', 'inp'))
- vis: bfloat16 [2, 64, 2048, 2048], P(None, ('freq', 'inp'), 'tm')
All inputs are finite; a program needn't handle non-finite values.
Results may differ from a plain program's by a relative error of at most 0.0034.
Values may be sent and summed in bfloat16 or wider, within the bound.
No kernel may reach another device: no remote copies, remote signals or barrier semaphores. Data moves between devices by JAX's collectives and lax.ppermute only.
A program may use at most 64 MiB of HBM per device.

v0:
```python
import math

import jax
import jax.numpy as jnp
from jax import lax
from jax.sharding import PartitionSpec as P


def from_behind(value, axis, by):
    count = lax.axis_size(axis)
    pairs = [(i, i + by) for i in range(count) if 0 <= i + by < count]
    return lax.ppermute(value, axis, pairs)


def cross_terms(rows, columns):
    depth = rows.shape[1]
    stacked_rows = rows.reshape((2 * depth,) + rows.shape[2:])
    real_cols = columns.reshape((2 * depth,) + columns.shape[2:])
    imag_cols = jnp.concatenate([columns[1], -columns[0]], axis=0)
    real_part = jnp.einsum(
        "nci,ncj->cij", stacked_rows, real_cols, preferred_element_type=jnp.float32
    )
    imag_part = jnp.einsum(
        "nci,ncj->cij", stacked_rows, imag_cols, preferred_element_type=jnp.float32
    )
    return (real_part, imag_part)


def body(volt, window):
    taps, chans = window.shape
    samples = volt.shape[1]
    width = volt.shape[2]
    frames = samples // chans
    series = volt.reshape(2, frames, chans, width)
    tail = series[:, frames - (taps - 1) :]
    prior = from_behind(tail, "tm", 1)
    extended = jnp.concatenate([prior, series], axis=1)
    filtered = window[0][None, None, :, None] * extended[:, taps - 1 : taps - 1 + frames]
    for j in range(1, taps):
        filtered = (
            filtered
            + window[j][None, None, :, None] * extended[:, taps - 1 - j : taps - 1 - j + frames]
        )
    group_size = chans // lax.axis_size("freq")
    channel_ids = lax.axis_index("freq") * group_size + jnp.arange(group_size, dtype=jnp.int32)
    positions = jnp.arange(chans, dtype=jnp.int32)
    phase = (positions[:, None] * channel_ids[None, :] % chans).astype(jnp.float32) * (
        2.0 * math.pi / chans
    )
    norm_factor = 1.0 / math.sqrt(chans)
    cosine = jnp.cos(phase) * norm_factor
    sine = jnp.sin(phase) * norm_factor
    table = jnp.stack([jnp.stack([cosine, -sine], axis=1), jnp.stack([sine, cosine], axis=1)])
    channelized = jnp.einsum(
        "pfka,pkqc->qfca",
        filtered,
        table,
        precision=lax.Precision.HIGHEST,
        preferred_element_type=jnp.float32,
    )
    local_spectra = channelized.astype(jnp.bfloat16)
    turned = lax.all_to_all(local_spectra, "inp", split_axis=2, concat_axis=3, tiled=True)
    blocks = lax.axis_size("tm")
    inputs = turned.shape[3]
    block_rows = inputs // blocks
    own_block = lax.axis_index("tm")
    scale = 1.0 / (frames * blocks)
    piece = lax.all_gather(turned, "tm", axis=1, tiled=True)
    rows = lax.dynamic_slice_in_dim(piece, own_block * block_rows, block_rows, 3)
    real_part, imag_part = cross_terms(rows, piece)
    vis = (jnp.stack([real_part, imag_part]) * scale).astype(jnp.bfloat16)
    return (turned, vis)


def solution(mesh):
    in_specs = (P(None, "tm", "inp"), P())
    out_specs = (P(None, "tm", ("freq", "inp"), None), P(None, ("freq", "inp"), "tm", None))
    return jax.shard_map(body, mesh=mesh, in_specs=in_specs, out_specs=out_specs, check_vma=False)
```

profile of v0, /device:TPU:24, one launch (start us, length us, event | category | flops | bytes accessed | tf_op | source)
XLA Modules:
  0.0 160.9 jit_solution(11049653130979218654)
XLA Ops:
  7.2 0.0 copy-start.1
  7.2 0.0 all-gather.2.cloned.1.call-start
  7.2 1.0 slice.40
  8.3 4.9 %collective-permute-start = (bf16[2,3,64,128]{3,2,0,1:T(8,128)(2,1)S(1)}, bf16[2,3,64,128]{3,2,0,1:T(8,128)(2,1)S(1)}, u32[]{:S(2)}, u32[]{:S(2)}) collective-permute-start(bf16[2,3,64,128]{3,2,0,1:T(8,128)(2,1)S(1)} %copy.34), channel_id=1, source_target_pairs={{0,4},{4,8},{8,12},{12,16},{16,20},{20,24},{24,28},{1,5},{5,9},{9,... | collective-permute-start | bytes 294920 | tf_op jit(solution)/shard_map/ppermute | solution.py:12
  13.2 0.8 slice_bitcast_fusion.4
  14.1 0.1 fusion.49
  14.2 3.0 %collective-permute-done = bf16[2,3,64,128]{3,2,0,1:T(8,128)(2,1)S(1)} collective-permute-done((bf16[2,3,64,128]{3,2,0,1:T(8,128)(2,1)S(1)}, bf16[2,3,64,128]{3,2,0,1:T(8,128)(2,1)S(1)}, u32[]{:S(2)}, u32[]{:S(2)}) %collective-permute-start) | collective-permute-done | bytes 98336 | tf_op jit(solution)/shard_map/ppermute | solution.py:12
  17.2 2.0 %constant_dynamic-update-slice_fusion = bf16[2,67,64,128]{3,2,0,1:T(8,128)(2,1)S(1)} fusion(bf16[2,67,64,128]{3,2,0,1:T(8,128)(2,1)S(1)} %constant_dynamic-update-slice_fusion.1, bf16[2,64,64,128]{3,2,1,0:T(8,128)(2,1)} %bitcast.69), kind=kLoop, calls=%fused_computation.53 | loop fusion | bytes 4194304 | tf_op jit(solution)/shard_map/concatenate | solution.py:37
  19.2 0.0 copy-done.1
  19.2 3.6 %fusion.37 = bf16[2,64,16,128]{3,2,1,0:T(8,128)(2,1)S(1)} fusion(bf16[2,67,64,128]{3,2,0,1:T(8,128)(2,1)S(1)} %constant_dynamic-update-slice_fusion, f32[64]{0:T(128)S(1)} %get-tuple-element.12, f32[64]{0:T(128)S(1)} %get-tuple-element.13, f32[64]{0:T(128)S(1)} %get-tuple-element.11, f32[64]{0:T(128)S(1)} %get-tuple-element.10, ...), kind=kOutput, calls=%fused_computation.35 | convolution fusion | flops 414453760 | bytes 8947712 | tf_op jit(solution)/shard_map/pfka,pkqc->qfca/dot_general | solution.py:54
  22.8 0.1 copy.21
  22.9 42.4 %all_to_all.12 = bf16[2,64,16,128]{3,1,0,2:T(8,128)(2,1)S(1)} all-to-all(bf16[2,64,16,128]{3,1,0,2:T(8,128)(2,1)S(1)} %copy.21), channel_id=1, replica_groups=mesh['inp'=16,'tm'=8,'freq'=4] {'inp'}, dimensions={2} | all-to-all | bytes 1048576 | tf_op jit(solution)/shard_map/all_to_all | solution.py:62
  65.3 0.3 copy.22
  65.7 1.0 all_to_all.10
  66.7 0.0 all-gather.2.cloned.1.call-update
  66.7 79.9 %all-gather.2.cloned.1.call-done = bf16[2,512,1,2048]{3,1,0,2:T(8,128)(2,1)} async-done(((bf16[2,64,1,2048]{3,1,0,2:T(8,128)(2,1)}), bf16[2,512,1,2048]{3,1,0,2:T(8,128)(2,1)}) %all-gather.2.cloned.1.call-update) | async-done | bytes 4194320 | tf_op jit(solution)/shard_map/all_gather | solution.py:68
  146.7 0.0 copy-start
  146.7 1.9 %slice_bitcast_fusion = bf16[512,1,2048]{2,0,1:T(8,128)(2,1)S(1)} fusion(bf16[2,512,1,2048]{3,1,2,0:T(8,128)(2,1)} %bitcast.67), kind=kLoop, calls=%fused_computation.25 | loop fusion | bytes 4194304 | tf_op jit(solution)/shard_map/squeeze | solution.py:19
  148.5 0.9 copy-done
  149.5 0.1 fusion.23
  149.6 0.1 constant_dynamic-slice_fusion
  149.7 1.3 fusion.19
  151.0 1.3 fusion.20
  152.2 1.8 %fusion.3 = bf16[2,1,256,2048]{3,2,1,0:T(8,128)(2,1)} fusion(f32[1,1,256,2048]{3,2,1,0:T(8,128)S(1)} %fusion.19, f32[1,1,256,2048]{3,2,1,0:T(8,128)S(1)} %fusion.20), kind=kLoop, calls=%fused_computation.5 | loop fusion | flops 3145728 | bytes 6291456 | tf_op jit(solution)/shard_map/convert_element_type | solution.py:71
  (4 shorter events, 0.0 us)
Async XLA Ops:
  7.2 12.0 %copy-start.1 = (bf16[2,4096,128]{2,1,0:T(8,128)(2,1)S(1)}, bf16[2,4096,128]{2,1,0:T(8,128)(2,1)}, u32[]{:S(2)}) copy-start(bf16[2,4096,128]{2,1,0:T(8,128)(2,1)} %param.2) | copy-start | bytes 6291460
  7.2 139.5 %all-gather.2.cloned.1.call-start = ((), (), s32[]{:S(2)}) async-start(), calls=%async_computation.1 | async-start | bytes 4718592 | tf_op jit(solution)/shard_map/all_gather | solution.py:68
  8.3 8.9 %collective-permute-start = (bf16[2,3,64,128]{3,2,0,1:T(8,128)(2,1)S(1)}, bf16[2,3,64,128]{3,2,0,1:T(8,128)(2,1)S(1)}, u32[]{:S(2)}, u32[]{:S(2)}) collective-permute-start(bf16[2,3,64,128]{3,2,0,1:T(8,128)(2,1)S(1)} %copy.34), channel_id=1, source_target_pairs={{0,4},{4,8},{8,12},{12,16},{16,20},{20,24},{24,28},{1,5},{5,9},{9,... | collective-permute-start | bytes 294920 | tf_op jit(solution)/shard_map/ppermute | solution.py:12
  146.7 2.8 %copy-start = (bf16[2,512,1,2048]{3,1,0,2:T(8,128)(2,1)S(1)}, bf16[2,512,1,2048]{3,1,0,2:T(8,128)(2,1)}, u32[]{:S(2)}) copy-start(bf16[2,512,1,2048]{3,1,0,2:T(8,128)(2,1)} %all-gather.2.cloned.1.call-done) | copy-start | bytes 12582916
Sparse Core Ops, SparseCore 0:
  66.8 79.7 all-gather.1
where the time goes:
time: 164 us; the launch traced here: 161 us
  waiting for transfers between devices  82.9 us (51%)
  blocking collectives  42.4 us (26%)
  between operations  14.1 us (9%)
  local copies, waits for them, and re-layouts  8.26 us (5%)
  matrix products  6.14 us (4%)
  starting transfers between devices  4.97 us (3%)
  other arithmetic  2.1 us (1%)
    all_gather x1, waiting for transfers between devices, body(): piece = lax.all_gather(turned, 'tm', axis=1, tiled=True)  79.9 us
    all_to_all x1, blocking collectives, body(): lax.all_to_all(local_spectra, 'inp', split_axis=2, concat_axis=3, tiled=T...  42.4 us
    ppermute x1, starting transfers between devices, from_behind(): return lax.ppermute(value, axis, pairs)  4.93 us
    dot_general x1, matrix products, body(): jnp.einsum('pfka,pkqc->qfca', filtered, table, precision=lax.Precision.HI...  3.61 us
  transfers between devices with their start and end apart: 2, of which 2 were waited for; matrix products, arithmetic and copies ran while one was open for 1% of the time, Pallas kernels for 0%

commit v1 on v0

--- a/solution.py
+++ b/solution.py
@@ -12,18 +12,26 @@
     return lax.ppermute(value, axis, pairs)
 
 
-def cross_terms(rows, columns):
-    depth = rows.shape[1]
-    stacked_rows = rows.reshape((2 * depth,) + rows.shape[2:])
-    real_cols = columns.reshape((2 * depth,) + columns.shape[2:])
-    imag_cols = jnp.concatenate([columns[1], -columns[0]], axis=0)
-    real_part = jnp.einsum(
-        "nci,ncj->cij", stacked_rows, real_cols, preferred_element_type=jnp.float32
-    )
-    imag_part = jnp.einsum(
-        "nci,ncj->cij", stacked_rows, imag_cols, preferred_element_type=jnp.float32
-    )
-    return (real_part, imag_part)
+def tm_shift(value, dy, dx):
+    ny = lax.axis_size("tm") // 2
+    pairs = [
+        (y * 2 + h, (y + dy) % ny * 2 + (h + dx) % 2) for y in range(ny) for h in range(2)
+    ]
+    return lax.ppermute(value, "tm", pairs)
+
+
+def gather_time(block):
+    half = block.shape[1] // 2
+    up = tm_shift(block, 1, 0)
+    down = tm_shift(block, -1, 0)
+    across = tm_shift(block, 0, 1)
+    far_a = tm_shift(up[:, :half], 1, 0)
+    far_b = tm_shift(down[:, half:], -1, 0)
+    far = jnp.concatenate([far_a, far_b], axis=1)
+    across_up = tm_shift(across, 1, 0)
+    across_down = tm_shift(across, -1, 0)
+    across_far = tm_shift(far, 0, 1)
+    return [block, up, down, across, far, across_up, across_down, across_far]
 
 
 def body(volt, window):
@@ -65,10 +73,16 @@
     block_rows = inputs // blocks
     own_block = lax.axis_index("tm")
     scale = 1.0 / (frames * blocks)
-    piece = lax.all_gather(turned, "tm", axis=1, tiled=True)
-    rows = lax.dynamic_slice_in_dim(piece, own_block * block_rows, block_rows, 3)
-    real_part, imag_part = cross_terms(rows, piece)
-    vis = (jnp.stack([real_part, imag_part]) * scale).astype(jnp.bfloat16)
+    pieces = gather_time(turned[:, :, 0])
+    columns = jnp.concatenate([p.reshape(2 * frames, inputs) for p in pieces], axis=0)
+    rows = lax.dynamic_slice_in_dim(columns, own_block * block_rows, block_rows, 1)
+    rows = rows.reshape(blocks, 2, frames, block_rows)
+    turned_rows = jnp.stack([-rows[:, 1], rows[:, 0]], axis=1)
+    left = jnp.concatenate([rows, turned_rows], axis=3).reshape(blocks * 2 * frames, 2 * block_rows)
+    product = lax.dot_general(
+        left, columns, (((0,), (0,)), ((), ())), preferred_element_type=jnp.float32
+    )
+    vis = (product * scale).astype(jnp.bfloat16).reshape(2, 1, block_rows, inputs)
     return (turned, vis)
 
 

time: 164 us -> 110 us (0.67)
  the two profiles are of different devices: /device:TPU:24 before, /device:TPU:2 now
where the time goes in v1:
time: 110 us
  blocking collectives  42.5 us (39%)
  starting transfers between devices  33.8 us (31%)
  local copies, waits for them, and re-layouts  13.4 us (12%)
  waiting for transfers between devices  9.62 us (9%)
  matrix products  9.51 us (9%)
    all_to_all x1, blocking collectives, body(): lax.all_to_all(local_spectra, 'inp', split_axis=2, concat_axis=3, tiled=T...  42.5 us
    ppermute x8, starting transfers between devices, tm_shift(): return lax.ppermute(value, 'tm', pairs)  29.8 us
    ppermute x8, waiting for transfers between devices, tm_shift(): return lax.ppermute(value, 'tm', pairs)  8.43 us
    unnamed x12, local copies, waits for them, and re-layouts  6 us
    dot_general x1, matrix products, body(): lax.dot_general(left, columns, (((0,), (0,)), ((), ())), preferred_elemen...  5.9 us
    ppermute x1, starting transfers between devices, from_behind(): return lax.ppermute(value, axis, pairs)  4.03 us
    dot_general x1, matrix products, body(): jnp.einsum('pfka,pkqc->qfca', filtered, table, precision=lax.Precision.HI...  3.61 us
  transfers between devices with their start and end apart: 9, of which 5 were waited for; matrix products, arithmetic and copies ran while one was open for 7% of the time, Pallas kernels for 0%

profile of v1, /device:TPU:2, one launch (start us, length us, event | category | flops | bytes accessed | tf_op | source)
XLA Modules:
  0.0 109.9 jit_solution(9508207953089697998)
XLA Ops:
  0.6 1.1 slice.48
  1.7 4.0 %collective-permute-start = (bf16[2,3,64,128]{3,2,0,1:T(8,128)(2,1)S(1)}, bf16[2,3,64,128]{3,2,0,1:T(8,128)(2,1)S(1)}, u32[]{:S(2)}, u32[]{:S(2)}) collective-permute-start(bf16[2,3,64,128]{3,2,0,1:T(8,128)(2,1)S(1)} %copy.37), channel_id=1, source_target_pairs={{0,4},{4,8},{8,12},{12,16},{16,20},{20,24},{24,28},{1,5},{5,9},{9,... | collective-permute-start | bytes 294920 | tf_op jit(solution)/shard_map/ppermute | solution.py:12
  6.7 1.2 %collective-permute-done = bf16[2,3,64,128]{3,2,0,1:T(8,128)(2,1)S(1)} collective-permute-done((bf16[2,3,64,128]{3,2,0,1:T(8,128)(2,1)S(1)}, bf16[2,3,64,128]{3,2,0,1:T(8,128)(2,1)S(1)}, u32[]{:S(2)}, u32[]{:S(2)}) %collective-permute-start) | collective-permute-done | bytes 98336 | tf_op jit(solution)/shard_map/ppermute | solution.py:12
  7.9 2.0 %constant_dynamic-update-slice_fusion = bf16[2,67,64,128]{3,2,0,1:T(8,128)(2,1)S(1)} fusion(bf16[2,67,64,128]{3,2,0,1:T(8,128)(2,1)S(1)} %constant_dynamic-update-slice_fusion.1, bf16[2,64,64,128]{3,2,1,0:T(8,128)(2,1)} %bitcast.65), kind=kLoop, calls=%fused_computation.34 | loop fusion | bytes 4194304 | tf_op jit(solution)/shard_map/concatenate | solution.py:45
  9.9 3.6 %fusion.26 = bf16[2,64,16,128]{3,2,1,0:T(8,128)(2,1)S(1)} fusion(bf16[2,67,64,128]{3,2,0,1:T(8,128)(2,1)S(1)} %constant_dynamic-update-slice_fusion, f32[64]{0:T(128)S(1)} %get-tuple-element.14, f32[64]{0:T(128)S(1)} %get-tuple-element.15, f32[64]{0:T(128)S(1)} %get-tuple-element.13, f32[64]{0:T(128)S(1)} %get-tuple-element.12, ...), kind=kOutput, calls=%fused_computation.23 | convolution fusion | flops 414453760 | bytes 8947712 | tf_op jit(solution)/shard_map/pfka,pkqc->qfca/dot_general | solution.py:62
  13.7 42.5 %all_to_all.12 = bf16[2,64,16,128]{3,1,0,2:T(8,128)(2,1)S(1)} all-to-all(bf16[2,64,16,128]{3,1,0,2:T(8,128)(2,1)S(1)} %copy.20), channel_id=1, replica_groups=mesh['inp'=16,'tm'=8,'freq'=4] {'inp'}, dimensions={2} | all-to-all | bytes 1048576 | tf_op jit(solution)/shard_map/all_to_all | solution.py:70
  56.3 6.1 %collective-permute-start.1 = (bf16[2,64,2048]{2,1,0:T(8,128)(2,1)S(1)}, bf16[2,64,2048]{2,1,0:T(8,128)(2,1)S(1)}, u32[]{:S(2)}, u32[]{:S(2)}) collective-permute-start(bf16[2,64,2048]{2,1,0:T(8,128)(2,1)S(1)} %copy_bitcast_fusion), channel_id=1, source_target_pairs={{0,8},{4,12},{8,16},{12,20},{16,24},{20,28},{24,0},{28,4},{1,9},{5... | collective-permute-start | bytes 1572872 | tf_op jit(solution)/shard_map/ppermute | solution.py:20
  62.3 3.4 %collective-permute-start.2 = (bf16[2,64,2048]{2,1,0:T(8,128)(2,1)S(1)}, bf16[2,64,2048]{2,1,0:T(8,128)(2,1)S(1)}, u32[]{:S(2)}, u32[]{:S(2)}) collective-permute-start(bf16[2,64,2048]{2,1,0:T(8,128)(2,1)S(1)} %copy_bitcast_fusion), channel_id=1, source_target_pairs={{0,24},{4,28},{8,0},{12,4},{16,8},{20,12},{24,16},{28,20},{1,25},{... | collective-permute-start | bytes 1572872 | tf_op jit(solution)/shard_map/ppermute | solution.py:20
  65.7 3.3 %collective-permute-start.3 = (bf16[2,64,2048]{2,1,0:T(8,128)(2,1)S(1)}, bf16[2,64,2048]{2,1,0:T(8,128)(2,1)S(1)}, u32[]{:S(2)}, u32[]{:S(2)}) collective-permute-start(bf16[2,64,2048]{2,1,0:T(8,128)(2,1)S(1)} %copy_bitcast_fusion), channel_id=1, source_target_pairs={{0,4},{4,0},{8,12},{12,8},{16,20},{20,16},{24,28},{28,24},{1,5},{5... | collective-permute-start | bytes 1572872 | tf_op jit(solution)/shard_map/ppermute | solution.py:20
  69.4 0.9 bitcast_dynamic-update-slice_fusion
  70.3 1.0 all_to_all.10
  71.3 1.1 collective-permute-done.1
  72.4 3.8 %collective-permute-start.4 = (bf16[2,32,2048]{2,1,0:T(8,128)(2,1)S(1)}, bf16[2,32,2048]{2,1,0:T(8,128)(2,1)S(1)}, u32[]{:S(2)}, u32[]{:S(2)}) collective-permute-start(bf16[2,32,2048]{2,1,0:T(8,128)(2,1)S(1)} %slice.52), channel_id=1, source_target_pairs={{0,8},{4,12},{8,16},{12,20},{16,24},{20,28},{24,0},{28,4},{1,9},{5... | collective-permute-start | bytes 786440 | tf_op jit(solution)/shard_map/ppermute | solution.py:20
  76.3 3.5 %collective-permute-start.5 = (bf16[2,32,2048]{2,1,0:T(8,128)(2,1)S(1)}, bf16[2,32,2048]{2,1,0:T(8,128)(2,1)S(1)}, u32[]{:S(2)}, u32[]{:S(2)}) collective-permute-start(bf16[2,32,2048]{2,1,0:T(8,128)(2,1)S(1)} %slice.53), channel_id=1, source_target_pairs={{0,24},{4,28},{8,0},{12,4},{16,8},{20,12},{24,16},{28,20},{1,25},{... | collective-permute-start | bytes 786440 | tf_op jit(solution)/shard_map/ppermute | solution.py:20
  80.6 0.9 constant_dynamic-update-slice_fusion.9
  82.3 2.4 %collective-permute-start.6 = (bf16[2,64,2048]{2,1,0:T(8,128)(2,1)S(1)}, bf16[2,64,2048]{2,1,0:T(8,128)(2,1)S(1)}, u32[]{:S(2)}, u32[]{:S(2)}) collective-permute-start(bf16[2,64,2048]{2,1,0:T(8,128)(2,1)S(1)} %collective-permute-done.3), channel_id=1, source_target_pairs={{0,8},{4,12},{8,16},{12,20},{16,24},{20,28},{24,0},{28,4},{1,9},{5... | collective-permute-start | bytes 1572872 | tf_op jit(solution)/shard_map/ppermute | solution.py:20
  84.7 4.7 %collective-permute-start.7 = (bf16[2,64,2048]{2,1,0:T(8,128)(2,1)S(1)}, bf16[2,64,2048]{2,1,0:T(8,128)(2,1)S(1)}, u32[]{:S(2)}, u32[]{:S(2)}) collective-permute-start(bf16[2,64,2048]{2,1,0:T(8,128)(2,1)S(1)} %collective-permute-done.3), channel_id=1, source_target_pairs={{0,24},{4,28},{8,0},{12,4},{16,8},{20,12},{24,16},{28,20},{1,25},{... | collective-permute-start | bytes 1572872 | tf_op jit(solution)/shard_map/ppermute | solution.py:20
  89.4 2.7 %collective-permute-start.8 = (bf16[2,64,2048]{2,1,0:T(8,128)(2,1)S(1)}, bf16[2,64,2048]{2,1,0:T(8,128)(2,1)S(1)}, u32[]{:S(2)}, u32[]{:S(2)}) collective-permute-start(bf16[2,64,2048]{2,1,0:T(8,128)(2,1)S(1)} %constant_dynamic-update-slice_fusion.2), channel_id=1, source_target_pairs={{0,4},{4,0},{8,12},{12,8},{16,20},{20,16},{24,28},{28,24},{1,5},{5... | collective-permute-start | bytes 1572872 | tf_op jit(solution)/shard_map/ppermute | solution.py:20
  93.0 1.6 %collective-permute-done.6 = bf16[2,64,2048]{2,1,0:T(8,128)(2,1)S(1)} collective-permute-done((bf16[2,64,2048]{2,1,0:T(8,128)(2,1)S(1)}, bf16[2,64,2048]{2,1,0:T(8,128)(2,1)S(1)}, u32[]{:S(2)}, u32[]{:S(2)}) %collective-permute-start.6) | collective-permute-done | bytes 524320 | tf_op jit(solution)/shard_map/ppermute | solution.py:20
  94.6 0.8 constant_dynamic-update-slice_fusion.6
  96.0 0.9 constant_dynamic-update-slice_fusion.5
  96.9 5.1 %collective-permute-done.8 = bf16[2,64,2048]{2,1,0:T(8,128)(2,1)S(1)} collective-permute-done((bf16[2,64,2048]{2,1,0:T(8,128)(2,1)S(1)}, bf16[2,64,2048]{2,1,0:T(8,128)(2,1)S(1)}, u32[]{:S(2)}, u32[]{:S(2)}) %collective-permute-start.8) | collective-permute-done | bytes 524320 | tf_op jit(solution)/shard_map/ppermute | solution.py:20
  102.8 1.1 constant_dynamic-slice_fusion
  104.0 5.9 %multiply_convert_fusion = bf16[512,2048]{1,0:T(8,128)(2,1)} fusion(bf16[1024,2048]{1,0:T(8,128)(2,1)} %constant_dynamic-update-slice_fusion.4, bf16[1024,256]{1,0:T(8,128)(2,1)S(1)} %bitcast.76, bf16[1024,256]{1,0:T(8,128)(2,1)S(1)} %constant_dynamic-slice_fusion), kind=kOutput, calls=%fused_computation.2 | convolution fusion | flops 2151677952 | bytes 7340032 | tf_op jit(solution)/shard_map/dot_general | solution.py:82
  (26 shorter events, 5.7 us)
Async XLA Ops:
  0.6 9.3 %copy-start = (bf16[2,4096,128]{2,1,0:T(8,128)(2,1)S(1)}, bf16[2,4096,128]{2,1,0:T(8,128)(2,1)}, u32[]{:S(2)}) copy-start(bf16[2,4096,128]{2,1,0:T(8,128)(2,1)} %param.2) | copy-start | bytes 6291460
  1.7 6.2 %collective-permute-start = (bf16[2,3,64,128]{3,2,0,1:T(8,128)(2,1)S(1)}, bf16[2,3,64,128]{3,2,0,1:T(8,128)(2,1)S(1)}, u32[]{:S(2)}, u32[]{:S(2)}) collective-permute-start(bf16[2,3,64,128]{3,2,0,1:T(8,128)(2,1)S(1)} %copy.37), channel_id=1, source_target_pairs={{0,4},{4,8},{8,12},{12,16},{16,20},{20,24},{24,28},{1,5},{5,9},{9,... | collective-permute-start | bytes 294920 | tf_op jit(solution)/shard_map/ppermute | solution.py:12
  56.3 16.1 %collective-permute-start.1 = (bf16[2,64,2048]{2,1,0:T(8,128)(2,1)S(1)}, bf16[2,64,2048]{2,1,0:T(8,128)(2,1)S(1)}, u32[]{:S(2)}, u32[]{:S(2)}) collective-permute-start(bf16[2,64,2048]{2,1,0:T(8,128)(2,1)S(1)} %copy_bitcast_fusion), channel_id=1, source_target_pairs={{0,8},{4,12},{8,16},{12,20},{16,24},{20,28},{24,0},{28,4},{1,9},{5... | collective-permute-start | bytes 1572872 | tf_op jit(solution)/shard_map/ppermute | solution.py:20
  62.3 13.9 %collective-permute-start.2 = (bf16[2,64,2048]{2,1,0:T(8,128)(2,1)S(1)}, bf16[2,64,2048]{2,1,0:T(8,128)(2,1)S(1)}, u32[]{:S(2)}, u32[]{:S(2)}) collective-permute-start(bf16[2,64,2048]{2,1,0:T(8,128)(2,1)S(1)} %copy_bitcast_fusion), channel_id=1, source_target_pairs={{0,24},{4,28},{8,0},{12,4},{16,8},{20,12},{24,16},{28,20},{1,25},{... | collective-permute-start | bytes 1572872 | tf_op jit(solution)/shard_map/ppermute | solution.py:20
  65.7 15.7 %collective-permute-start.3 = (bf16[2,64,2048]{2,1,0:T(8,128)(2,1)S(1)}, bf16[2,64,2048]{2,1,0:T(8,128)(2,1)S(1)}, u32[]{:S(2)}, u32[]{:S(2)}) collective-permute-start(bf16[2,64,2048]{2,1,0:T(8,128)(2,1)S(1)} %copy_bitcast_fusion), channel_id=1, source_target_pairs={{0,4},{4,0},{8,12},{12,8},{16,20},{20,16},{24,28},{28,24},{1,5},{5... | collective-permute-start | bytes 1572872 | tf_op jit(solution)/shard_map/ppermute | solution.py:20
  72.4 16.9 %collective-permute-start.4 = (bf16[2,32,2048]{2,1,0:T(8,128)(2,1)S(1)}, bf16[2,32,2048]{2,1,0:T(8,128)(2,1)S(1)}, u32[]{:S(2)}, u32[]{:S(2)}) collective-permute-start(bf16[2,32,2048]{2,1,0:T(8,128)(2,1)S(1)} %slice.52), channel_id=1, source_target_pairs={{0,8},{4,12},{8,16},{12,20},{16,24},{20,28},{24,0},{28,4},{1,9},{5... | collective-permute-start | bytes 786440 | tf_op jit(solution)/shard_map/ppermute | solution.py:20
  76.3 13.1 %collective-permute-start.5 = (bf16[2,32,2048]{2,1,0:T(8,128)(2,1)S(1)}, bf16[2,32,2048]{2,1,0:T(8,128)(2,1)S(1)}, u32[]{:S(2)}, u32[]{:S(2)}) collective-permute-start(bf16[2,32,2048]{2,1,0:T(8,128)(2,1)S(1)} %slice.53), channel_id=1, source_target_pairs={{0,24},{4,28},{8,0},{12,4},{16,8},{20,12},{24,16},{28,20},{1,25},{... | collective-permute-start | bytes 786440 | tf_op jit(solution)/shard_map/ppermute | solution.py:20
  82.3 12.3 %collective-permute-start.6 = (bf16[2,64,2048]{2,1,0:T(8,128)(2,1)S(1)}, bf16[2,64,2048]{2,1,0:T(8,128)(2,1)S(1)}, u32[]{:S(2)}, u32[]{:S(2)}) collective-permute-start(bf16[2,64,2048]{2,1,0:T(8,128)(2,1)S(1)} %collective-permute-done.3), channel_id=1, source_target_pairs={{0,8},{4,12},{8,16},{12,20},{16,24},{20,28},{24,0},{28,4},{1,9},{5... | collective-permute-start | bytes 1572872 | tf_op jit(solution)/shard_map/ppermute | solution.py:20
  84.7 11.4 %collective-permute-start.7 = (bf16[2,64,2048]{2,1,0:T(8,128)(2,1)S(1)}, bf16[2,64,2048]{2,1,0:T(8,128)(2,1)S(1)}, u32[]{:S(2)}, u32[]{:S(2)}) collective-permute-start(bf16[2,64,2048]{2,1,0:T(8,128)(2,1)S(1)} %collective-permute-done.3), channel_id=1, source_target_pairs={{0,24},{4,28},{8,0},{12,4},{16,8},{20,12},{24,16},{28,20},{1,25},{... | collective-permute-start | bytes 1572872 | tf_op jit(solution)/shard_map/ppermute | solution.py:20
  89.4 12.6 %collective-permute-start.8 = (bf16[2,64,2048]{2,1,0:T(8,128)(2,1)S(1)}, bf16[2,64,2048]{2,1,0:T(8,128)(2,1)S(1)}, u32[]{:S(2)}, u32[]{:S(2)}) collective-permute-start(bf16[2,64,2048]{2,1,0:T(8,128)(2,1)S(1)} %constant_dynamic-update-slice_fusion.2), channel_id=1, source_target_pairs={{0,4},{4,0},{8,12},{12,8},{16,20},{20,16},{24,28},{28,24},{1,5},{5... | collective-permute-start | bytes 1572872 | tf_op jit(solution)/shard_map/ppermute | solution.py:20

commit v2 on v1

v2 whole, which is shorter than its diff:
```python
import functools
import math

import jax
import jax.numpy as jnp
import numpy as np
from jax import lax
from jax.experimental import pallas as pl
from jax.experimental.pallas import tpu as pltpu
from jax.sharding import PartitionSpec as P

VM = pl.BlockSpec(memory_space=pltpu.VMEM)
SM = pl.BlockSpec(memory_space=pltpu.SMEM)
HB = pl.BlockSpec(memory_space=pltpu.HBM)
LOAD_LIMIT = 50 << 20
PARAMS = pltpu.CompilerParams(vmem_limit_bytes=16 << 20)


def from_behind(value, axis, by):
    count = lax.axis_size(axis)
    pairs = [(i, i + by) for i in range(count) if 0 <= i + by < count]
    return lax.ppermute(value, axis, pairs)


def tm_shift(value, dy, dx):
    ny = lax.axis_size("tm") // 2
    pairs = [
        (y * 2 + h, (y + dy) % ny * 2 + (h + dx) % 2) for y in range(ny) for h in range(2)
    ]
    return lax.ppermute(value, "tm", pairs)


def shares_of(taps, table_ref, frames):
    rows = table_ref.shape[0] // (2 * taps)
    width = frames[0][0].shape[1]
    x = jnp.concatenate([jnp.concatenate([p[0], p[1]], axis=0) for p in frames], axis=1)
    y = jnp.dot(table_ref[...], x, preferred_element_type=jnp.float32)
    parts = []
    for j in range(taps):
        at = 2 * j * rows
        parts.append(y[at : at + rows] + y[at + rows : at + 2 * rows])
    return [[part[:, s * width : (s + 1) * width] for part in parts] for s in range(len(frames))]


def advance(carry, share):
    sums = [c + s for c, s in zip(carry, share)] + [share[-1]]
    return sums[0], tuple(sums[1:])


def load_kernel(volt_ref, tail_ref, held_ref, sems):
    chunks = sems.shape[0] - 1
    samples = volt_ref.shape[1]
    span = samples // chunks
    last = tail_ref.shape[1]
    copies = [pltpu.make_async_copy(volt_ref.at[:, samples - last :], tail_ref, sems.at[chunks])]
    for i in range(chunks):
        part = slice(i * span, (i + 1) * span)
        copies.append(pltpu.make_async_copy(volt_ref.at[:, part], held_ref.at[:, part], sems.at[i]))
    for copy in copies:
        copy.start()
    for copy in copies:
        copy.wait()


def load(volt, last):
    return pl.pallas_call(
        load_kernel,
        out_shape=(
            jax.ShapeDtypeStruct((volt.shape[0], last, volt.shape[2]), volt.dtype),
            jax.ShapeDtypeStruct(volt.shape, volt.dtype),
        ),
        in_specs=[HB],
        out_specs=(VM, VM),
        scratch_shapes=[pltpu.SemaphoreType.DMA((5,))],
        cost_estimate=pl.CostEstimate(flops=0, bytes_accessed=4 * volt.size, transcendentals=0),
        compiler_params=pltpu.CompilerParams(vmem_limit_bytes=LOAD_LIMIT),
        name="load",
    )(volt)


def main_kernel(taps, _, table_ref, window_ref, volt_ref, out_ref, open_ref, split_ref):
    frames, rows, width = out_ref.shape
    chans = volt_ref.shape[1] // frames
    halo = taps - 1
    step = 8

    def frame_of(f):
        at = f * chans if isinstance(f, int) else pl.multiple_of(f * chans, chans)
        return [volt_ref[p, pl.ds(at, chans), :] for p in range(2)]

    base = table_ref[...]
    for j in range(taps):
        weights = window_ref[j : j + 1, :]
        tapped = base * jnp.concatenate([weights, weights], axis=1)
        coarse = tapped.astype(jnp.bfloat16)
        at = 2 * j * rows
        split_ref[at : at + rows, :] = coarse
        split_ref[at + rows : at + 2 * rows, :] = (tapped - coarse.astype(jnp.float32)).astype(jnp.bfloat16)

    def block(i, carry):
        every = []
        for s in range(0, step, 2):
            every += shares_of(taps, split_ref, [frame_of(i * step + s), frame_of(i * step + s + 1)])
        for s, share in enumerate(every):
            done, carry = advance(carry, share)
            out_ref[i * step + s] = done.astype(out_ref.dtype)
            if isinstance(i, int) and s < halo:
                open_ref[s] = done
        return carry

    carry = block(0, tuple(jnp.zeros((rows, width), jnp.float32) for _ in range(halo)))
    lax.fori_loop(1, frames // step, block, carry)


def head_kernel(taps, table_ref, prior_ref, open_ref, main_ref, out_ref):
    rows, width = out_ref.shape[1:]
    halo = taps - 1
    chans = prior_ref.shape[1] // halo
    frames = [[prior_ref[p, f * chans : (f + 1) * chans, :] for p in range(2)] for f in range(halo)]
    carry = tuple(jnp.zeros((rows, width), jnp.float32) for _ in range(halo))
    for share in shares_of(taps, table_ref, frames):
        _, carry = advance(carry, share)
    for f in range(halo):
        out_ref[f] = (open_ref[f] + carry[f]).astype(out_ref.dtype)


def dft_table(chans, group_size):
    channel = np.arange(chans).reshape(-1, group_size)
    phase = channel[:, :, None] * np.arange(chans) % chans * (2.0 * math.pi / chans)
    cosine = np.cos(phase) / math.sqrt(chans)
    sine = np.sin(phase) / math.sqrt(chans)
    real = np.concatenate([cosine, sine], axis=2)
    imag = np.concatenate([-sine, cosine], axis=2)
    return np.concatenate([real, imag], axis=1).astype(np.float32)


def channelize(held, prior, window, group, groups, frames):
    taps, chans = window.shape
    rows = 2 * chans // groups
    width = held.shape[2]
    table = jnp.asarray(dft_table(chans, chans // groups))
    local, open_sums, split = pl.pallas_call(
        functools.partial(main_kernel, taps),
        out_shape=(
            jax.ShapeDtypeStruct((frames, rows, width), jnp.bfloat16),
            jax.ShapeDtypeStruct((taps - 1, rows, width), jnp.float32),
            jax.ShapeDtypeStruct((taps * 2 * rows, 2 * chans), jnp.bfloat16),
        ),
        grid_spec=pltpu.PrefetchScalarGridSpec(
            num_scalar_prefetch=1,
            grid=(1,),
            in_specs=[
                pl.BlockSpec((None, rows, 2 * chans), lambda i, group: (group[0], 0, 0)),
                VM,
                VM,
            ],
            out_specs=(VM, VM, VM),
        ),
        cost_estimate=pl.CostEstimate(
            flops=4 * rows * taps * held.size, bytes_accessed=3 * held.size, transcendentals=0
        ),
        compiler_params=PARAMS,
        name="channelize",
    )(group, table, window, held)
    return pl.pallas_call(
        functools.partial(head_kernel, taps),
        out_shape=jax.ShapeDtypeStruct(local.shape, local.dtype),
        in_specs=[VM] * 4,
        out_specs=VM,
        input_output_aliases={3: 0},
        cost_estimate=pl.CostEstimate(
            flops=4 * rows * taps * prior.size, bytes_accessed=3 * prior.size, transcendentals=0
        ),
        compiler_params=PARAMS,
        name="channelize_head",
    )(split, prior, open_sums, local)


def fill_left(left_ref, at, piece, first, parts):
    blocks = [piece[first + s] for s in range(parts)]
    rows = jnp.concatenate([jnp.concatenate([b[0], b[1]], axis=0) for b in blocks], axis=1)
    turned = jnp.concatenate([jnp.concatenate([-b[1], b[0]], axis=0) for b in blocks], axis=1)
    both = jnp.concatenate([rows, turned], axis=1)
    left_ref[:, at : at + both.shape[0]] = both.T


def column_tile(pieces, z, wide):
    tall = []
    for piece in pieces:
        across = [piece[z + s] for s in range(wide)]
        across = [jnp.concatenate([b[0], b[1]], axis=0) for b in across]
        tall.append(jnp.concatenate(across, axis=1))
    return jnp.concatenate(tall, axis=0)


def spectra_kernel(block_ref, spectra_ref, token_ref, sems):
    token_ref[...] = jnp.zeros_like(token_ref)
    zs, _, _, width = block_ref.shape
    copies = []
    for z in range(zs):
        cols = slice(z * width, (z + 1) * width)
        copies.append(pltpu.make_async_copy(block_ref.at[z], spectra_ref.at[:, :, cols], sems.at[z]))
        copies[-1].start()
    for copy in copies:
        copy.wait()


def first_kernel(wide, own_ref, *refs):
    *pieces, total_ref, left_ref = refs
    zs, _, frames, width = pieces[0].shape
    parts = left_ref.shape[0] // (2 * width)
    for i, piece in enumerate(pieces):
        fill_left(left_ref, 2 * frames * i, piece, own_ref[0] * parts, parts)
    for z in range(0, zs, wide):
        total_ref[:, z * width : (z + wide) * width] = jnp.dot(
            left_ref[...], column_tile(pieces, z, wide), preferred_element_type=jnp.float32
        )


def more_kernel(wide, own_ref, before_ref, *refs):
    *pieces, total_ref, left_ref = refs
    zs, _, frames, width = pieces[0].shape
    parts = left_ref.shape[0] // (2 * width)
    for i, piece in enumerate(pieces):
        fill_left(left_ref, 2 * frames * i, piece, own_ref[0] * parts, parts)
    for z in range(0, zs, wide):
        cols = slice(z * width, (z + wide) * width)
        total_ref[:, cols] = before_ref[:, cols] + jnp.dot(
            left_ref[...], column_tile(pieces, z, wide), preferred_element_type=jnp.float32
        )


def last_kernel(wide, scale, own_ref, total_ref, low_ref, high_ref, vis_ref, left_ref, out_ref, sems):
    cut, _, frames, width = low_ref.shape
    zs = cut + high_ref.shape[0]
    rows = out_ref.shape[1]
    parts = rows // width
    first = own_ref[0] * parts

    @pl.when(first < cut)
    def _():
        fill_left(left_ref, 0, low_ref, first, parts)

    @pl.when(first >= cut)
    def _():
        fill_left(left_ref, 0, high_ref, first - cut, parts)

    copies = []
    for i, z in enumerate(range(0, zs, wide)):
        piece, at = (low_ref, z) if z < cut else (high_ref, z - cut)
        cols = slice(z * width, (z + wide) * width)
        product = jnp.dot(
            left_ref[...], column_tile([piece], at, wide), preferred_element_type=jnp.float32
        )
        out = ((product + total_ref[:, cols]) * scale).astype(out_ref.dtype)
        out_ref[0, :, cols] = out[:rows]
        out_ref[1, :, cols] = out[rows:]
        copies.append(
            pltpu.make_async_copy(out_ref.at[:, :, cols], vis_ref.at[:, :, cols], sems.at[i])
        )
        copies[-1].start()
    for copy in copies:
        copy.wait()


def spectra_of(block):
    zs, _, frames, width = block.shape
    return pl.pallas_call(
        spectra_kernel,
        out_shape=(
            jax.ShapeDtypeStruct((2, frames, zs * width), jnp.bfloat16),
            jax.ShapeDtypeStruct((8, 128), jnp.float32),
        ),
        in_specs=[VM],
        out_specs=(HB, VM),
        scratch_shapes=[pltpu.SemaphoreType.DMA((zs,))],
        cost_estimate=pl.CostEstimate(flops=0, bytes_accessed=4 * block.size, transcendentals=0),
        compiler_params=PARAMS,
        name="spectra_out",
    )(block)


def vis_first(own, pieces, rows):
    zs, _, frames, width = pieces[0].shape
    cols = zs * width
    depth = 2 * frames * len(pieces)
    return pl.pallas_call(
        functools.partial(first_kernel, 2),
        out_shape=jax.ShapeDtypeStruct((2 * rows, cols), jnp.float32),
        in_specs=[SM] + [VM] * len(pieces),
        out_specs=VM,
        scratch_shapes=[pltpu.VMEM((2 * rows, depth), jnp.bfloat16)],
        cost_estimate=pl.CostEstimate(
            flops=4 * rows * cols * depth, bytes_accessed=8 * rows * cols, transcendentals=0
        ),
        compiler_params=PARAMS,
        name="vis_first",
    )(own, *pieces)


def vis_more(own, total, pieces, rows):
    zs, _, frames, width = pieces[0].shape
    cols = zs * width
    depth = 2 * frames * len(pieces)
    return pl.pallas_call(
        functools.partial(more_kernel, 2),
        out_shape=jax.ShapeDtypeStruct((2 * rows, cols), jnp.float32),
        in_specs=[SM, VM] + [VM] * len(pieces),
        out_specs=VM,
        scratch_shapes=[pltpu.VMEM((2 * rows, depth), jnp.bfloat16)],
        input_output_aliases={1: 0},
        cost_estimate=pl.CostEstimate(
            flops=4 * rows * cols * depth, bytes_accessed=8 * rows * cols, transcendentals=0
        ),
        compiler_params=PARAMS,
        name="vis_more",
    )(own, total, *pieces)


def vis_last(own, total, low, high, rows, scale):
    frames, width = low.shape[2:]
    zs = low.shape[0] + high.shape[0]
    cols = zs * width
    wide = 2
    return pl.pallas_call(
        functools.partial(last_kernel, wide, scale),
        out_shape=jax.ShapeDtypeStruct((2, rows, cols), jnp.bfloat16),
        in_specs=[SM, VM, VM, VM],
        out_specs=HB,
        scratch_shapes=[
            pltpu.VMEM((2 * rows, 2 * frames), jnp.bfloat16),
            pltpu.VMEM((2, rows, cols), jnp.bfloat16),
            pltpu.SemaphoreType.DMA((zs // wide,)),
        ],
        cost_estimate=pl.CostEstimate(
            flops=8 * rows * cols * frames, bytes_accessed=8 * rows * cols, transcendentals=0
        ),
        compiler_params=PARAMS,
        name="vis_last",
    )(own, total, low, high)


def after_kernel(*refs):
    pass


def after(other, *values):
    count = len(values)
    return pl.pallas_call(
        after_kernel,
        out_shape=tuple(jax.ShapeDtypeStruct(v.shape, v.dtype) for v in values),
        in_specs=[VM] * count + [pl.BlockSpec(memory_space=pl.ANY)],
        out_specs=(VM,) * count,
        input_output_aliases={i: i for i in range(count)},
        compiler_params=PARAMS,
        name="after",
    )(*values, other)


def correlate(block, own, rows, scale):
    cut = block.shape[0] * 5 // 16 * 2
    up = tm_shift(block, 1, 0)
    across = tm_shift(block, 0, 1)
    down = tm_shift(block, -1, 0)
    spectra, written = spectra_of(block)
    (up,) = after(written, up)
    far = tm_shift(up, 1, 0)
    across_up = tm_shift(up, 0, 1)
    across, down = after(written, across, down)
    across_down = tm_shift(across, -1, 0)
    total = vis_first(own, [block, up, across, down], rows)
    (far,) = after(total, far)
    last_low = tm_shift(far[:cut], 0, 1)
    last_high = tm_shift(across_up[cut:], 1, 0)
    total = vis_more(own, total, [far, across_up, across_down], rows)
    return spectra, vis_last(own, total, last_low, last_high, rows, scale)


def body(volt, window):
    taps, chans = window.shape
    samples, width = volt.shape[1:]
    frames = samples // chans
    tail, held = load(volt, (taps - 1) * chans)
    prior = from_behind(tail, "tm", 1)
    groups = lax.axis_size("freq")
    group = lax.axis_index("freq").astype(jnp.int32).reshape(1)
    local = channelize(held, prior, window, group, groups, frames)
    local = jnp.transpose(local.reshape(frames, 2, chans // groups, width), (2, 1, 0, 3))
    block = lax.all_to_all(local, "inp", split_axis=0, concat_axis=0, tiled=True)
    inputs = block.shape[0] * width
    blocks = lax.axis_size("tm")
    own = lax.axis_index("tm").astype(jnp.int32).reshape(1)
    spectra, vis = correlate(block, own, inputs // blocks, 1.0 / (frames * blocks))
    return (spectra[:, :, None], vis[:, None])


def solution(mesh):
    in_specs = (P(None, "tm", "inp"), P())
    out_specs = (P(None, "tm", ("freq", "inp"), None), P(None, ("freq", "inp"), "tm", None))
    return jax.shard_map(body, mesh=mesh, in_specs=in_specs, out_specs=out_specs, check_vma=False)
```

time: 110 us -> 98.1 us (0.89)
  the two profiles are of different devices: /device:TPU:2 before, /device:TPU:32 now
where the time goes in v2:
time: 98.1 us; the launch traced here: 97.6 us
  blocking collectives  42.7 us (44%)
  starting transfers between devices  35.2 us (36%)
  Pallas kernels  10.7 us (11%)
  waiting for transfers between devices  7.92 us (8%)
    all_to_all x1, blocking collectives, body(): lax.all_to_all(local, 'inp', split_axis=0, concat_axis=0, tiled=True)  42.7 us
    ppermute x8, starting transfers between devices, tm_shift(): return lax.ppermute(value, 'tm', pairs)  30.3 us
    ppermute x8, waiting for transfers between devices, tm_shift(): return lax.ppermute(value, 'tm', pairs)  7.92 us
    ppermute x1, starting transfers between devices, from_behind(): return lax.ppermute(value, axis, pairs)  4.93 us
    pallas_call x1, Pallas kernels, channelize(): pl.pallas_call(functools.partial(main_kernel, taps), out_shape=(jax.Shape...  2.46 us
    pallas_call x1, Pallas kernels, vis_more(): pl.pallas_call(functools.partial(more_kernel, 2), out_shape=jax.ShapeDtyp...  2.42 us
  transfers between devices with their start and end apart: 9, of which 4 were waited for; matrix products, arithmetic and copies ran while one was open for 0% of the time, Pallas kernels for 7%

profile of v2, /device:TPU:32, one launch (start us, length us, event | category | flops | bytes accessed | tf_op | source)
XLA Modules:
  0.0 97.6 jit_solution(377746706743789943)
XLA Ops:
  0.6 0.0 copy-start
  0.7 1.6 %load.1 = (bf16[2,192,128]{2,1,0:T(8,128)(2,1)S(1)}, bf16[2,4096,128]{2,1,0:T(8,128)(2,1)S(1)}) custom-call(bf16[2,4096,128]{2,1,0:T(8,128)(2,1)} %volt_ref.1), custom_call_target="tpu_custom_call" | custom-call | bytes 4194304 | tf_op jit(solution)/shard_map/load/pallas_call | solution.py:66
  2.3 4.9 %collective-permute-start = (bf16[2,192,128]{2,1,0:T(8,128)(2,1)S(1)}, bf16[2,192,128]{2,1,0:T(8,128)(2,1)S(1)}, u32[]{:S(2)}, u32[]{:S(2)}) collective-permute-start(bf16[2,192,128]{2,1,0:T(8,128)(2,1)S(1)} %get-tuple-element.13), channel_id=1, source_target_pairs={{0,4},{4,8},{8,12},{12,16},{16,20},{20,24},{24,28},{1,5},{5,9},{9,... | collective-permute-start | bytes 294920 | tf_op jit(solution)/shard_map/ppermute | solution.py:22
  7.3 2.5 %channelize.1 = (bf16[64,32,128]{2,1,0:T(8,128)(2,1)S(1)}, f32[3,32,128]{2,1,0:T(8,128)S(1)}, bf16[256,128]{1,0:T(8,128)(2,1)S(1)}) custom-call(s32[1]{0:T(128)} %bitcast._, f32[4,32,128]{2,1,0:T(8,128)S(1)} %copy-done, f32[4,64]{1,0:T(4,128)S(1)} %copy-done.1, bf16[2,4096,128]{2,1,0:T(8,128)(2,1)S(1)} %get-tuple-element.11.volt_ref), custom_call_target="tpu_custom_call" | custom-call | flops 536870912 | bytes 3145728 | tf_op jit(solution)/shard_map/channelize/pallas_call | solution.py:142
  9.7 0.0 collective-permute-done.prior_ref
  9.7 0.2 channelize_head.1
  10.0 0.2 copy.17
  10.2 42.7 %all_to_all.5.block_ref.refs_0_ = bf16[16,2,64,128]{3,2,1,0:T(8,128)(2,1)S(1)} all-to-all(bf16[16,2,64,128]{3,2,1,0:T(8,128)(2,1)S(1)} %bitcast.14), channel_id=1, replica_groups=mesh['inp'=16,'tm'=8,'freq'=4] {'inp'}, dimensions={0} | all-to-all | bytes 1048576 | tf_op jit(solution)/shard_map/all_to_all | solution.py:389
  52.9 4.9 %collective-permute-start.1 = (bf16[16,2,64,128]{3,2,1,0:T(8,128)(2,1)S(1)}, bf16[16,2,64,128]{3,2,1,0:T(8,128)(2,1)S(1)}, u32[]{:S(2)}, u32[]{:S(2)}) collective-permute-start(bf16[16,2,64,128]{3,2,1,0:T(8,128)(2,1)S(1)} %all_to_all.5.block_ref.refs_0_), channel_id=1, source_target_pairs={{0,8},{4,12},{8,16},{12,20},{16,24},{20,28},{24,0},{28,4},{1,9},{5... | collective-permute-start | bytes 1572872 | tf_op jit(solution)/shard_map/ppermute | solution.py:30
  57.8 4.0 %collective-permute-start.2 = (bf16[16,2,64,128]{3,2,1,0:T(8,128)(2,1)S(1)}, bf16[16,2,64,128]{3,2,1,0:T(8,128)(2,1)S(1)}, u32[]{:S(2)}, u32[]{:S(2)}) collective-permute-start(bf16[16,2,64,128]{3,2,1,0:T(8,128)(2,1)S(1)} %all_to_all.5.block_ref.refs_0_), channel_id=1, source_target_pairs={{0,4},{4,0},{8,12},{12,8},{16,20},{20,16},{24,28},{28,24},{1,5},{5... | collective-permute-start | bytes 1572872 | tf_op jit(solution)/shard_map/ppermute | solution.py:30
  61.8 3.6 %collective-permute-start.3 = (bf16[16,2,64,128]{3,2,1,0:T(8,128)(2,1)S(1)}, bf16[16,2,64,128]{3,2,1,0:T(8,128)(2,1)S(1)}, u32[]{:S(2)}, u32[]{:S(2)}) collective-permute-start(bf16[16,2,64,128]{3,2,1,0:T(8,128)(2,1)S(1)} %all_to_all.5.block_ref.refs_0_), channel_id=1, source_target_pairs={{0,24},{4,28},{8,0},{12,4},{16,8},{20,12},{24,16},{28,20},{1,25},{... | collective-permute-start | bytes 1572872 | tf_op jit(solution)/shard_map/ppermute | solution.py:30
  65.4 0.9 spectra_out.1
  66.3 0.7 collective-permute-done.1.refs_0_
  67.0 4.0 %collective-permute-start.4 = (bf16[16,2,64,128]{3,2,1,0:T(8,128)(2,1)S(1)}, bf16[16,2,64,128]{3,2,1,0:T(8,128)(2,1)S(1)}, u32[]{:S(2)}, u32[]{:S(2)}) collective-permute-start(bf16[16,2,64,128]{3,2,1,0:T(8,128)(2,1)S(1)} %after.3.refs_1_), channel_id=1, source_target_pairs={{0,8},{4,12},{8,16},{12,20},{16,24},{20,28},{24,0},{28,4},{1,9},{5... | collective-permute-start | bytes 1572872 | tf_op jit(solution)/shard_map/ppermute | solution.py:30
  71.0 4.1 %collective-permute-start.5 = (bf16[16,2,64,128]{3,2,1,0:T(8,128)(2,1)S(1)}, bf16[16,2,64,128]{3,2,1,0:T(8,128)(2,1)S(1)}, u32[]{:S(2)}, u32[]{:S(2)}) collective-permute-start(bf16[16,2,64,128]{3,2,1,0:T(8,128)(2,1)S(1)} %after.3.refs_1_), channel_id=1, source_target_pairs={{0,4},{4,0},{8,12},{12,8},{16,20},{20,16},{24,28},{28,24},{1,5},{5... | collective-permute-start | bytes 1572872 | tf_op jit(solution)/shard_map/ppermute | solution.py:30
  75.1 0.3 collective-permute-done.3.refs_1_
  75.4 3.5 %collective-permute-start.6 = (bf16[16,2,64,128]{3,2,1,0:T(8,128)(2,1)S(1)}, bf16[16,2,64,128]{3,2,1,0:T(8,128)(2,1)}, u32[]{:S(2)}, u32[]{:S(2)}) collective-permute-start(bf16[16,2,64,128]{3,2,1,0:T(8,128)(2,1)S(1)} %get-tuple-element.18.refs_2_), channel_id=1, source_target_pairs={{0,24},{4,28},{8,0},{12,4},{16,8},{20,12},{24,16},{28,20},{1,25},{... | collective-permute-start | bytes 1572872 | tf_op jit(solution)/shard_map/ppermute | solution.py:30
  78.9 1.3 %vis_first.1.refs_1_.before_ref = f32[512,2048]{1,0:T(8,128)S(1)} custom-call(s32[1]{0:T(128)} %bitcast.5.own_ref, bf16[16,2,64,128]{3,2,1,0:T(8,128)(2,1)S(1)} %all_to_all.5.block_ref.refs_0_, bf16[16,2,64,128]{3,2,1,0:T(8,128)(2,1)S(1)} %after.3.refs_1_, bf16[16,2,64,128]{3,2,1,0:T(8,128)(2,1)S(1)} %get-tuple-element.18.refs_2_, ...), custom_call_target="tpu_custom_call" | custom-call | flops 1073741824 | bytes 4194304 | tf_op jit(solution)/shard_map/vis_first/pallas_call | solution.py:287
  80.2 3.6 %collective-permute-start.7 = (bf16[10,2,64,128]{3,2,1,0:T(8,128)(2,1)S(1)}, bf16[10,2,64,128]{3,2,1,0:T(8,128)(2,1)S(1)}, u32[]{:S(2)}, u32[]{:S(2)}) collective-permute-start(bf16[10,2,64,128]{3,2,1,0:T(8,128)(2,1)S(1)} %slice.8), channel_id=1, source_target_pairs={{0,4},{4,0},{8,12},{12,8},{16,20},{20,16},{24,28},{28,24},{1,5},{5... | collective-permute-start | bytes 983048 | tf_op jit(solution)/shard_map/ppermute | solution.py:30
  83.9 3.2 %collective-permute-done.5.refs_1_ = bf16[16,2,64,128]{3,2,1,0:T(8,128)(2,1)S(1)} collective-permute-done((bf16[16,2,64,128]{3,2,1,0:T(8,128)(2,1)S(1)}, bf16[16,2,64,128]{3,2,1,0:T(8,128)(2,1)S(1)}, u32[]{:S(2)}, u32[]{:S(2)}) %collective-permute-start.5) | collective-permute-done | bytes 524320 | tf_op jit(solution)/shard_map/ppermute | solution.py:30
  87.1 2.6 %collective-permute-start.8 = (bf16[6,2,64,128]{3,2,1,0:T(8,128)(2,1)S(1)}, bf16[6,2,64,128]{3,2,1,0:T(8,128)(2,1)S(1)}, u32[]{:S(2)}, u32[]{:S(2)}) collective-permute-start(bf16[6,2,64,128]{3,2,1,0:T(8,128)(2,1)S(1)} %slice.9), channel_id=1, source_target_pairs={{0,8},{4,12},{8,16},{12,20},{16,24},{20,28},{24,0},{28,4},{1,9},{5... | collective-permute-start | bytes 589832 | tf_op jit(solution)/shard_map/ppermute | solution.py:30
  89.7 2.4 %vis_more.1.total_ref = f32[512,2048]{1,0:T(8,128)S(1)} custom-call(s32[1]{0:T(128)} %bitcast.5.own_ref, f32[512,2048]{1,0:T(8,128)S(1)} %vis_first.1.refs_1_.before_ref, bf16[16,2,64,128]{3,2,1,0:T(8,128)(2,1)S(1)} %after.5.refs_0_, bf16[16,2,64,128]{3,2,1,0:T(8,128)(2,1)S(1)} %collective-permute-done.5.refs_1_, ...), custom_call_target="tpu_custom_call", output_to_operand_aliasing={{}: (1, {})} | custom-call | flops 805306368 | bytes 4194304 | tf_op jit(solution)/shard_map/vis_more/pallas_call | solution.py:305
  92.2 3.7 %collective-permute-done.8.high_ref = bf16[6,2,64,128]{3,2,1,0:T(8,128)(2,1)S(1)} collective-permute-done((bf16[6,2,64,128]{3,2,1,0:T(8,128)(2,1)S(1)}, bf16[6,2,64,128]{3,2,1,0:T(8,128)(2,1)S(1)}, u32[]{:S(2)}, u32[]{:S(2)}) %collective-permute-start.8) | collective-permute-done | bytes 196640 | tf_op jit(solution)/shard_map/ppermute | solution.py:30
  95.9 1.8 %vis_last.1 = bf16[2,256,2048]{2,1,0:T(8,128)(2,1)} custom-call(s32[1]{0:T(128)} %bitcast.5.own_ref, f32[512,2048]{1,0:T(8,128)S(1)} %vis_more.1.total_ref, bf16[10,2,64,128]{3,2,1,0:T(8,128)(2,1)S(1)} %collective-permute-done.7.low_ref, bf16[6,2,64,128]{3,2,1,0:T(8,128)(2,1)S(1)} %collective-permute-done.8.high_ref), custom_call_target="tpu_custom_call" | custom-call | flops 268435456 | bytes 4194304 | tf_op jit(solution)/shard_map/vis_last/pallas_call | solution.py:325
  (12 shorter events, 0.1 us)
Async XLA Ops:
  0.6 6.6 %copy-start = (f32[4,32,128]{2,1,0:T(8,128)S(1)}, f32[4,32,128]{2,1,0:T(8,128)}, u32[]{:S(2)}) copy-start(f32[4,32,128]{2,1,0:T(8,128)} %constant.11.clone.table_ref) | copy-start | bytes 196612
  0.6 6.6 %copy-start.1 = (f32[4,64]{1,0:T(4,128)S(1)}, f32[4,64]{1,0:T(4,128)}, u32[]{:S(2)}) copy-start(f32[4,64]{1,0:T(4,128)} %window_ref.1) | copy-start | bytes 3076
  2.3 7.4 %collective-permute-start = (bf16[2,192,128]{2,1,0:T(8,128)(2,1)S(1)}, bf16[2,192,128]{2,1,0:T(8,128)(2,1)S(1)}, u32[]{:S(2)}, u32[]{:S(2)}) collective-permute-start(bf16[2,192,128]{2,1,0:T(8,128)(2,1)S(1)} %get-tuple-element.13), channel_id=1, source_target_pairs={{0,4},{4,8},{8,12},{12,16},{16,20},{20,24},{24,28},{1,5},{5,9},{9,... | collective-permute-start | bytes 294920 | tf_op jit(solution)/shard_map/ppermute | solution.py:22
  52.9 14.2 %collective-permute-start.1 = (bf16[16,2,64,128]{3,2,1,0:T(8,128)(2,1)S(1)}, bf16[16,2,64,128]{3,2,1,0:T(8,128)(2,1)S(1)}, u32[]{:S(2)}, u32[]{:S(2)}) collective-permute-start(bf16[16,2,64,128]{3,2,1,0:T(8,128)(2,1)S(1)} %all_to_all.5.block_ref.refs_0_), channel_id=1, source_target_pairs={{0,8},{4,12},{8,16},{12,20},{16,24},{20,28},{24,0},{28,4},{1,9},{5... | collective-permute-start | bytes 1572872 | tf_op jit(solution)/shard_map/ppermute | solution.py:30
  57.8 17.4 %collective-permute-start.2 = (bf16[16,2,64,128]{3,2,1,0:T(8,128)(2,1)S(1)}, bf16[16,2,64,128]{3,2,1,0:T(8,128)(2,1)S(1)}, u32[]{:S(2)}, u32[]{:S(2)}) collective-permute-start(bf16[16,2,64,128]{3,2,1,0:T(8,128)(2,1)S(1)} %all_to_all.5.block_ref.refs_0_), channel_id=1, source_target_pairs={{0,4},{4,0},{8,12},{12,8},{16,20},{20,16},{24,28},{28,24},{1,5},{5... | collective-permute-start | bytes 1572872 | tf_op jit(solution)/shard_map/ppermute | solution.py:30
  61.8 13.6 %collective-permute-start.3 = (bf16[16,2,64,128]{3,2,1,0:T(8,128)(2,1)S(1)}, bf16[16,2,64,128]{3,2,1,0:T(8,128)(2,1)S(1)}, u32[]{:S(2)}, u32[]{:S(2)}) collective-permute-start(bf16[16,2,64,128]{3,2,1,0:T(8,128)(2,1)S(1)} %all_to_all.5.block_ref.refs_0_), channel_id=1, source_target_pairs={{0,24},{4,28},{8,0},{12,4},{16,8},{20,12},{24,16},{28,20},{1,25},{... | collective-permute-start | bytes 1572872 | tf_op jit(solution)/shard_map/ppermute | solution.py:30
  67.0 13.2 %collective-permute-start.4 = (bf16[16,2,64,128]{3,2,1,0:T(8,128)(2,1)S(1)}, bf16[16,2,64,128]{3,2,1,0:T(8,128)(2,1)S(1)}, u32[]{:S(2)}, u32[]{:S(2)}) collective-permute-start(bf16[16,2,64,128]{3,2,1,0:T(8,128)(2,1)S(1)} %after.3.refs_1_), channel_id=1, source_target_pairs={{0,8},{4,12},{8,16},{12,20},{16,24},{20,28},{24,0},{28,4},{1,9},{5... | collective-permute-start | bytes 1572872 | tf_op jit(solution)/shard_map/ppermute | solution.py:30
  71.0 16.1 %collective-permute-start.5 = (bf16[16,2,64,128]{3,2,1,0:T(8,128)(2,1)S(1)}, bf16[16,2,64,128]{3,2,1,0:T(8,128)(2,1)S(1)}, u32[]{:S(2)}, u32[]{:S(2)}) collective-permute-start(bf16[16,2,64,128]{3,2,1,0:T(8,128)(2,1)S(1)} %after.3.refs_1_), channel_id=1, source_target_pairs={{0,4},{4,0},{8,12},{12,8},{16,20},{20,16},{24,28},{28,24},{1,5},{5... | collective-permute-start | bytes 1572872 | tf_op jit(solution)/shard_map/ppermute | solution.py:30
  75.4 14.3 %collective-permute-start.6 = (bf16[16,2,64,128]{3,2,1,0:T(8,128)(2,1)S(1)}, bf16[16,2,64,128]{3,2,1,0:T(8,128)(2,1)}, u32[]{:S(2)}, u32[]{:S(2)}) collective-permute-start(bf16[16,2,64,128]{3,2,1,0:T(8,128)(2,1)S(1)} %get-tuple-element.18.refs_2_), channel_id=1, source_target_pairs={{0,24},{4,28},{8,0},{12,4},{16,8},{20,12},{24,16},{28,20},{1,25},{... | collective-permute-start | bytes 1572872 | tf_op jit(solution)/shard_map/ppermute | solution.py:30
  80.2 15.6 %collective-permute-start.7 = (bf16[10,2,64,128]{3,2,1,0:T(8,128)(2,1)S(1)}, bf16[10,2,64,128]{3,2,1,0:T(8,128)(2,1)S(1)}, u32[]{:S(2)}, u32[]{:S(2)}) collective-permute-start(bf16[10,2,64,128]{3,2,1,0:T(8,128)(2,1)S(1)} %slice.8), channel_id=1, source_target_pairs={{0,4},{4,0},{8,12},{12,8},{16,20},{20,16},{24,28},{28,24},{1,5},{5... | collective-permute-start | bytes 983048 | tf_op jit(solution)/shard_map/ppermute | solution.py:30
  87.1 8.8 %collective-permute-start.8 = (bf16[6,2,64,128]{3,2,1,0:T(8,128)(2,1)S(1)}, bf16[6,2,64,128]{3,2,1,0:T(8,128)(2,1)S(1)}, u32[]{:S(2)}, u32[]{:S(2)}) collective-permute-start(bf16[6,2,64,128]{3,2,1,0:T(8,128)(2,1)S(1)} %slice.9), channel_id=1, source_target_pairs={{0,8},{4,12},{8,16},{12,20},{16,24},{20,28},{24,0},{28,4},{1,9},{5... | collective-permute-start | bytes 589832 | tf_op jit(solution)/shard_map/ppermute | solution.py:30

commit v3 on v2

--- a/solution.py
+++ b/solution.py
@@ -16,16 +16,20 @@
 PARAMS = pltpu.CompilerParams(vmem_limit_bytes=16 << 20)
 
 
-def from_behind(value, axis, by):
-    count = lax.axis_size(axis)
-    pairs = [(i, i + by) for i in range(count) if 0 <= i + by < count]
-    return lax.ppermute(value, axis, pairs)
+def from_behind(value):
+    count, groups = lax.axis_size("tm"), lax.axis_size("freq")
+    pairs = [
+        (t * groups + (f ^ (groups // 2)), (t + 1) * groups + f)
+        for t in range(count - 1)
+        for f in range(groups)
+    ]
+    return lax.ppermute(value, ("tm", "freq"), pairs)
 
 
 def tm_shift(value, dy, dx):
     ny = lax.axis_size("tm") // 2
     pairs = [
-        (y * 2 + h, (y + dy) % ny * 2 + (h + dx) % 2) for y in range(ny) for h in range(2)
+        (y * 2 + h, (y - dy) % ny * 2 + (h + dx) % 2) for y in range(ny) for h in range(2)
     ]
     return lax.ppermute(value, "tm", pairs)
 
@@ -358,7 +362,7 @@
 
 
 def correlate(block, own, rows, scale):
-    cut = block.shape[0] * 5 // 16 * 2
+    cut = block.shape[0] * 4 // 16 * 2
     up = tm_shift(block, 1, 0)
     across = tm_shift(block, 0, 1)
     down = tm_shift(block, -1, 0)
@@ -381,7 +385,7 @@
     samples, width = volt.shape[1:]
     frames = samples // chans
     tail, held = load(volt, (taps - 1) * chans)
-    prior = from_behind(tail, "tm", 1)
+    prior = from_behind(tail)
     groups = lax.axis_size("freq")
     group = lax.axis_index("freq").astype(jnp.int32).reshape(1)
     local = channelize(held, prior, window, group, groups, frames)

time: 98.1 us -> 97.3 us (level)
  the two profiles are of different devices: /device:TPU:32 before, /device:TPU:24 now
where the time goes in v3:
time: 97.3 us; the launch traced here: 96.9 us
  blocking collectives  42.4 us (44%)
  starting transfers between devices  29.3 us (30%)
  waiting for transfers between devices  13.5 us (14%)
  Pallas kernels  10.7 us (11%)
    all_to_all x1, blocking collectives, body(): lax.all_to_all(local, 'inp', split_axis=0, concat_axis=0, tiled=True)  42.4 us
    ppermute x8, starting transfers between devices, tm_shift(): return lax.ppermute(value, 'tm', pairs)  24.6 us
    ppermute x8, waiting for transfers between devices, tm_shift(): return lax.ppermute(value, 'tm', pairs)  12 us
    ppermute x1, starting transfers between devices, from_behind(): return lax.ppermute(value, ('tm', 'freq'), pairs)  4.67 us
    pallas_call x1, Pallas kernels, channelize(): pl.pallas_call(functools.partial(main_kernel, taps), out_shape=(jax.Shape...  2.46 us
    pallas_call x1, Pallas kernels, vis_more(): pl.pallas_call(functools.partial(more_kernel, 2), out_shape=jax.ShapeDtyp...  2.42 us
  transfers between devices with their start and end apart: 9, of which 7 were waited for; matrix products, arithmetic and copies ran while one was open for 0% of the time, Pallas kernels for 7%

profile of v3, /device:TPU:24, one launch (start us, length us, event | category | flops | bytes accessed | tf_op | source)
XLA Modules:
  0.0 96.9 jit_solution(16788546447509569098)
XLA Ops:
  0.7 1.6 %load.1 = (bf16[2,192,128]{2,1,0:T(8,128)(2,1)S(1)}, bf16[2,4096,128]{2,1,0:T(8,128)(2,1)S(1)}) custom-call(bf16[2,4096,128]{2,1,0:T(8,128)(2,1)} %volt_ref.1), custom_call_target="tpu_custom_call" | custom-call | bytes 4194304 | tf_op jit(solution)/shard_map/load/pallas_call | solution.py:70
  2.3 4.7 %collective-permute-start = (bf16[2,192,128]{2,1,0:T(8,128)(2,1)S(1)}, bf16[2,192,128]{2,1,0:T(8,128)(2,1)S(1)}, u32[]{:S(2)}, u32[]{:S(2)}) collective-permute-start(bf16[2,192,128]{2,1,0:T(8,128)(2,1)S(1)} %get-tuple-element.13), channel_id=1, source_target_pairs={{2,4},{3,5},{0,6},{1,7},{6,8},{7,9},{4,10},{5,11},{10,12},{11,13},... | collective-permute-start | bytes 294920 | tf_op jit(solution)/shard_map/ppermute | solution.py:26
  7.0 2.5 %channelize.1 = (bf16[64,32,128]{2,1,0:T(8,128)(2,1)S(1)}, f32[3,32,128]{2,1,0:T(8,128)S(1)}, bf16[256,128]{1,0:T(8,128)(2,1)S(1)}) custom-call(s32[1]{0:T(128)} %bitcast._, f32[4,32,128]{2,1,0:T(8,128)S(1)} %copy-done, f32[4,64]{1,0:T(4,128)S(1)} %copy-done.1, bf16[2,4096,128]{2,1,0:T(8,128)(2,1)S(1)} %get-tuple-element.11.volt_ref), custom_call_target="tpu_custom_call" | custom-call | flops 536870912 | bytes 3145728 | tf_op jit(solution)/shard_map/channelize/pallas_call | solution.py:146
  9.5 1.5 %collective-permute-done.prior_ref = bf16[2,192,128]{2,1,0:T(8,128)(2,1)S(1)} collective-permute-done((bf16[2,192,128]{2,1,0:T(8,128)(2,1)S(1)}, bf16[2,192,128]{2,1,0:T(8,128)(2,1)S(1)}, u32[]{:S(2)}, u32[]{:S(2)}) %collective-permute-start) | collective-permute-done | bytes 98336 | tf_op jit(solution)/shard_map/ppermute | solution.py:26
  11.1 0.2 copy.17
  11.3 42.4 %all_to_all.5.block_ref.refs_0_ = bf16[16,2,64,128]{3,2,1,0:T(8,128)(2,1)S(1)} all-to-all(bf16[16,2,64,128]{3,2,1,0:T(8,128)(2,1)S(1)} %bitcast.14), channel_id=1, replica_groups=mesh['inp'=16,'tm'=8,'freq'=4] {'inp'}, dimensions={0} | all-to-all | bytes 1048576 | tf_op jit(solution)/shard_map/all_to_all | solution.py:393
  53.7 2.6 %collective-permute-start.1 = (bf16[16,2,64,128]{3,2,1,0:T(8,128)(2,1)S(1)}, bf16[16,2,64,128]{3,2,1,0:T(8,128)(2,1)S(1)}, u32[]{:S(2)}, u32[]{:S(2)}) collective-permute-start(bf16[16,2,64,128]{3,2,1,0:T(8,128)(2,1)S(1)} %all_to_all.5.block_ref.refs_0_), channel_id=1, source_target_pairs={{0,24},{4,28},{8,0},{12,4},{16,8},{20,12},{24,16},{28,20},{1,25},{... | collective-permute-start | bytes 1572872 | tf_op jit(solution)/shard_map/ppermute | solution.py:34
  56.4 2.8 %collective-permute-start.2 = (bf16[16,2,64,128]{3,2,1,0:T(8,128)(2,1)S(1)}, bf16[16,2,64,128]{3,2,1,0:T(8,128)(2,1)S(1)}, u32[]{:S(2)}, u32[]{:S(2)}) collective-permute-start(bf16[16,2,64,128]{3,2,1,0:T(8,128)(2,1)S(1)} %all_to_all.5.block_ref.refs_0_), channel_id=1, source_target_pairs={{0,4},{4,0},{8,12},{12,8},{16,20},{20,16},{24,28},{28,24},{1,5},{5... | collective-permute-start | bytes 1572872 | tf_op jit(solution)/shard_map/ppermute | solution.py:34
  59.2 4.4 %collective-permute-start.3 = (bf16[16,2,64,128]{3,2,1,0:T(8,128)(2,1)S(1)}, bf16[16,2,64,128]{3,2,1,0:T(8,128)(2,1)S(1)}, u32[]{:S(2)}, u32[]{:S(2)}) collective-permute-start(bf16[16,2,64,128]{3,2,1,0:T(8,128)(2,1)S(1)} %all_to_all.5.block_ref.refs_0_), channel_id=1, source_target_pairs={{0,8},{4,12},{8,16},{12,20},{16,24},{20,28},{24,0},{28,4},{1,9},{5... | collective-permute-start | bytes 1572872 | tf_op jit(solution)/shard_map/ppermute | solution.py:34
  63.6 0.9 spectra_out.1
  64.5 3.8 %collective-permute-done.1.refs_0_ = bf16[16,2,64,128]{3,2,1,0:T(8,128)(2,1)S(1)} collective-permute-done((bf16[16,2,64,128]{3,2,1,0:T(8,128)(2,1)S(1)}, bf16[16,2,64,128]{3,2,1,0:T(8,128)(2,1)S(1)}, u32[]{:S(2)}, u32[]{:S(2)}) %collective-permute-start.1) | collective-permute-done | bytes 524320 | tf_op jit(solution)/shard_map/ppermute | solution.py:34
  68.3 1.9 %collective-permute-start.4 = (bf16[16,2,64,128]{3,2,1,0:T(8,128)(2,1)S(1)}, bf16[16,2,64,128]{3,2,1,0:T(8,128)(2,1)S(1)}, u32[]{:S(2)}, u32[]{:S(2)}) collective-permute-start(bf16[16,2,64,128]{3,2,1,0:T(8,128)(2,1)S(1)} %after.3.refs_1_), channel_id=1, source_target_pairs={{0,24},{4,28},{8,0},{12,4},{16,8},{20,12},{24,16},{28,20},{1,25},{... | collective-permute-start | bytes 1572872 | tf_op jit(solution)/shard_map/ppermute | solution.py:34
  70.2 2.3 %collective-permute-start.5 = (bf16[16,2,64,128]{3,2,1,0:T(8,128)(2,1)S(1)}, bf16[16,2,64,128]{3,2,1,0:T(8,128)(2,1)S(1)}, u32[]{:S(2)}, u32[]{:S(2)}) collective-permute-start(bf16[16,2,64,128]{3,2,1,0:T(8,128)(2,1)S(1)} %after.3.refs_1_), channel_id=1, source_target_pairs={{0,4},{4,0},{8,12},{12,8},{16,20},{20,16},{24,28},{28,24},{1,5},{5... | collective-permute-start | bytes 1572872 | tf_op jit(solution)/shard_map/ppermute | solution.py:34
  72.5 0.5 collective-permute-done.3.refs_1_
  73.0 5.1 %collective-permute-start.6 = (bf16[16,2,64,128]{3,2,1,0:T(8,128)(2,1)S(1)}, bf16[16,2,64,128]{3,2,1,0:T(8,128)(2,1)}, u32[]{:S(2)}, u32[]{:S(2)}) collective-permute-start(bf16[16,2,64,128]{3,2,1,0:T(8,128)(2,1)S(1)} %get-tuple-element.18.refs_2_), channel_id=1, source_target_pairs={{0,8},{4,12},{8,16},{12,20},{16,24},{20,28},{24,0},{28,4},{1,9},{5... | collective-permute-start | bytes 1572872 | tf_op jit(solution)/shard_map/ppermute | solution.py:34
  78.2 1.3 %vis_first.1.refs_1_.before_ref = f32[512,2048]{1,0:T(8,128)S(1)} custom-call(s32[1]{0:T(128)} %bitcast.5.own_ref, bf16[16,2,64,128]{3,2,1,0:T(8,128)(2,1)S(1)} %all_to_all.5.block_ref.refs_0_, bf16[16,2,64,128]{3,2,1,0:T(8,128)(2,1)S(1)} %after.3.refs_1_, bf16[16,2,64,128]{3,2,1,0:T(8,128)(2,1)S(1)} %get-tuple-element.18.refs_2_, ...), custom_call_target="tpu_custom_call" | custom-call | flops 1073741824 | bytes 4194304 | tf_op jit(solution)/shard_map/vis_first/pallas_call | solution.py:291
  79.5 1.6 %collective-permute-done.4.refs_0_ = bf16[16,2,64,128]{3,2,1,0:T(8,128)(2,1)S(1)} collective-permute-done((bf16[16,2,64,128]{3,2,1,0:T(8,128)(2,1)S(1)}, bf16[16,2,64,128]{3,2,1,0:T(8,128)(2,1)S(1)}, u32[]{:S(2)}, u32[]{:S(2)}) %collective-permute-start.4) | collective-permute-done | bytes 524320 | tf_op jit(solution)/shard_map/ppermute | solution.py:34
  81.0 3.5 %collective-permute-start.7 = (bf16[8,2,64,128]{3,2,1,0:T(8,128)(2,1)S(1)}, bf16[8,2,64,128]{3,2,1,0:T(8,128)(2,1)S(1)}, u32[]{:S(2)}, u32[]{:S(2)}) collective-permute-start(bf16[8,2,64,128]{3,2,1,0:T(8,128)(2,1)S(1)} %slice.8), channel_id=1, source_target_pairs={{0,4},{4,0},{8,12},{12,8},{16,20},{20,16},{24,28},{28,24},{1,5},{5... | collective-permute-start | bytes 786440 | tf_op jit(solution)/shard_map/ppermute | solution.py:34
  84.5 1.1 %collective-permute-done.5.refs_1_ = bf16[16,2,64,128]{3,2,1,0:T(8,128)(2,1)S(1)} collective-permute-done((bf16[16,2,64,128]{3,2,1,0:T(8,128)(2,1)S(1)}, bf16[16,2,64,128]{3,2,1,0:T(8,128)(2,1)S(1)}, u32[]{:S(2)}, u32[]{:S(2)}) %collective-permute-start.5) | collective-permute-done | bytes 524320 | tf_op jit(solution)/shard_map/ppermute | solution.py:34
  85.6 2.0 %collective-permute-start.8 = (bf16[8,2,64,128]{3,2,1,0:T(8,128)(2,1)S(1)}, bf16[8,2,64,128]{3,2,1,0:T(8,128)(2,1)S(1)}, u32[]{:S(2)}, u32[]{:S(2)}) collective-permute-start(bf16[8,2,64,128]{3,2,1,0:T(8,128)(2,1)S(1)} %slice.9), channel_id=1, source_target_pairs={{0,24},{4,28},{8,0},{12,4},{16,8},{20,12},{24,16},{28,20},{1,25},{... | collective-permute-start | bytes 786440 | tf_op jit(solution)/shard_map/ppermute | solution.py:34
  87.7 2.4 %vis_more.1.total_ref = f32[512,2048]{1,0:T(8,128)S(1)} custom-call(s32[1]{0:T(128)} %bitcast.5.own_ref, f32[512,2048]{1,0:T(8,128)S(1)} %vis_first.1.refs_1_.before_ref, bf16[16,2,64,128]{3,2,1,0:T(8,128)(2,1)S(1)} %after.5.refs_0_, bf16[16,2,64,128]{3,2,1,0:T(8,128)(2,1)S(1)} %collective-permute-done.5.refs_1_, ...), custom_call_target="tpu_custom_call", output_to_operand_aliasing={{}: (1, {})} | custom-call | flops 805306368 | bytes 4194304 | tf_op jit(solution)/shard_map/vis_more/pallas_call | solution.py:309
  90.1 0.7 collective-permute-done.7.low_ref
  90.8 4.3 %collective-permute-done.8.high_ref = bf16[8,2,64,128]{3,2,1,0:T(8,128)(2,1)S(1)} collective-permute-done((bf16[8,2,64,128]{3,2,1,0:T(8,128)(2,1)S(1)}, bf16[8,2,64,128]{3,2,1,0:T(8,128)(2,1)S(1)}, u32[]{:S(2)}, u32[]{:S(2)}) %collective-permute-start.8) | collective-permute-done | bytes 262176 | tf_op jit(solution)/shard_map/ppermute | solution.py:34
  95.1 1.8 %vis_last.1 = bf16[2,256,2048]{2,1,0:T(8,128)(2,1)} custom-call(s32[1]{0:T(128)} %bitcast.5.own_ref, f32[512,2048]{1,0:T(8,128)S(1)} %vis_more.1.total_ref, bf16[8,2,64,128]{3,2,1,0:T(8,128)(2,1)S(1)} %collective-permute-done.7.low_ref, bf16[8,2,64,128]{3,2,1,0:T(8,128)(2,1)S(1)} %collective-permute-done.8.high_ref), custom_call_target="tpu_custom_call" | custom-call | flops 268435456 | bytes 4194304 | tf_op jit(solution)/shard_map/vis_last/pallas_call | solution.py:329
  (12 shorter events, 0.3 us)
Async XLA Ops:
  0.6 6.4 %copy-start = (f32[4,32,128]{2,1,0:T(8,128)S(1)}, f32[4,32,128]{2,1,0:T(8,128)}, u32[]{:S(2)}) copy-start(f32[4,32,128]{2,1,0:T(8,128)} %constant.11.clone.table_ref) | copy-start | bytes 196612
  0.6 6.3 %copy-start.1 = (f32[4,64]{1,0:T(4,128)S(1)}, f32[4,64]{1,0:T(4,128)}, u32[]{:S(2)}) copy-start(f32[4,64]{1,0:T(4,128)} %window_ref.1) | copy-start | bytes 3076
  2.3 8.6 %collective-permute-start = (bf16[2,192,128]{2,1,0:T(8,128)(2,1)S(1)}, bf16[2,192,128]{2,1,0:T(8,128)(2,1)S(1)}, u32[]{:S(2)}, u32[]{:S(2)}) collective-permute-start(bf16[2,192,128]{2,1,0:T(8,128)(2,1)S(1)} %get-tuple-element.13), channel_id=1, source_target_pairs={{2,4},{3,5},{0,6},{1,7},{6,8},{7,9},{4,10},{5,11},{10,12},{11,13},... | collective-permute-start | bytes 294920 | tf_op jit(solution)/shard_map/ppermute | solution.py:26
  53.7 14.6 %collective-permute-start.1 = (bf16[16,2,64,128]{3,2,1,0:T(8,128)(2,1)S(1)}, bf16[16,2,64,128]{3,2,1,0:T(8,128)(2,1)S(1)}, u32[]{:S(2)}, u32[]{:S(2)}) collective-permute-start(bf16[16,2,64,128]{3,2,1,0:T(8,128)(2,1)S(1)} %all_to_all.5.block_ref.refs_0_), channel_id=1, source_target_pairs={{0,24},{4,28},{8,0},{12,4},{16,8},{20,12},{24,16},{28,20},{1,25},{... | collective-permute-start | bytes 1572872 | tf_op jit(solution)/shard_map/ppermute | solution.py:34
  56.4 16.1 %collective-permute-start.2 = (bf16[16,2,64,128]{3,2,1,0:T(8,128)(2,1)S(1)}, bf16[16,2,64,128]{3,2,1,0:T(8,128)(2,1)S(1)}, u32[]{:S(2)}, u32[]{:S(2)}) collective-permute-start(bf16[16,2,64,128]{3,2,1,0:T(8,128)(2,1)S(1)} %all_to_all.5.block_ref.refs_0_), channel_id=1, source_target_pairs={{0,4},{4,0},{8,12},{12,8},{16,20},{20,16},{24,28},{28,24},{1,5},{5... | collective-permute-start | bytes 1572872 | tf_op jit(solution)/shard_map/ppermute | solution.py:34
  59.2 13.8 %collective-permute-start.3 = (bf16[16,2,64,128]{3,2,1,0:T(8,128)(2,1)S(1)}, bf16[16,2,64,128]{3,2,1,0:T(8,128)(2,1)S(1)}, u32[]{:S(2)}, u32[]{:S(2)}) collective-permute-start(bf16[16,2,64,128]{3,2,1,0:T(8,128)(2,1)S(1)} %all_to_all.5.block_ref.refs_0_), channel_id=1, source_target_pairs={{0,8},{4,12},{8,16},{12,20},{16,24},{20,28},{24,0},{28,4},{1,9},{5... | collective-permute-start | bytes 1572872 | tf_op jit(solution)/shard_map/ppermute | solution.py:34
  68.3 12.7 %collective-permute-start.4 = (bf16[16,2,64,128]{3,2,1,0:T(8,128)(2,1)S(1)}, bf16[16,2,64,128]{3,2,1,0:T(8,128)(2,1)S(1)}, u32[]{:S(2)}, u32[]{:S(2)}) collective-permute-start(bf16[16,2,64,128]{3,2,1,0:T(8,128)(2,1)S(1)} %after.3.refs_1_), channel_id=1, source_target_pairs={{0,24},{4,28},{8,0},{12,4},{16,8},{20,12},{24,16},{28,20},{1,25},{... | collective-permute-start | bytes 1572872 | tf_op jit(solution)/shard_map/ppermute | solution.py:34
  70.2 15.4 %collective-permute-start.5 = (bf16[16,2,64,128]{3,2,1,0:T(8,128)(2,1)S(1)}, bf16[16,2,64,128]{3,2,1,0:T(8,128)(2,1)S(1)}, u32[]{:S(2)}, u32[]{:S(2)}) collective-permute-start(bf16[16,2,64,128]{3,2,1,0:T(8,128)(2,1)S(1)} %after.3.refs_1_), channel_id=1, source_target_pairs={{0,4},{4,0},{8,12},{12,8},{16,20},{20,16},{24,28},{28,24},{1,5},{5... | collective-permute-start | bytes 1572872 | tf_op jit(solution)/shard_map/ppermute | solution.py:34
  73.0 14.6 %collective-permute-start.6 = (bf16[16,2,64,128]{3,2,1,0:T(8,128)(2,1)S(1)}, bf16[16,2,64,128]{3,2,1,0:T(8,128)(2,1)}, u32[]{:S(2)}, u32[]{:S(2)}) collective-permute-start(bf16[16,2,64,128]{3,2,1,0:T(8,128)(2,1)S(1)} %get-tuple-element.18.refs_2_), channel_id=1, source_target_pairs={{0,8},{4,12},{8,16},{12,20},{16,24},{20,28},{24,0},{28,4},{1,9},{5... | collective-permute-start | bytes 1572872 | tf_op jit(solution)/shard_map/ppermute | solution.py:34
  81.0 9.8 %collective-permute-start.7 = (bf16[8,2,64,128]{3,2,1,0:T(8,128)(2,1)S(1)}, bf16[8,2,64,128]{3,2,1,0:T(8,128)(2,1)S(1)}, u32[]{:S(2)}, u32[]{:S(2)}) collective-permute-start(bf16[8,2,64,128]{3,2,1,0:T(8,128)(2,1)S(1)} %slice.8), channel_id=1, source_target_pairs={{0,4},{4,0},{8,12},{12,8},{16,20},{20,16},{24,28},{28,24},{1,5},{5... | collective-permute-start | bytes 786440 | tf_op jit(solution)/shard_map/ppermute | solution.py:34
  85.6 9.5 %collective-permute-start.8 = (bf16[8,2,64,128]{3,2,1,0:T(8,128)(2,1)S(1)}, bf16[8,2,64,128]{3,2,1,0:T(8,128)(2,1)S(1)}, u32[]{:S(2)}, u32[]{:S(2)}) collective-permute-start(bf16[8,2,64,128]{3,2,1,0:T(8,128)(2,1)S(1)} %slice.9), channel_id=1, source_target_pairs={{0,24},{4,28},{8,0},{12,4},{16,8},{20,12},{24,16},{28,20},{1,25},{... | collective-permute-start | bytes 786440 | tf_op jit(solution)/shard_map/ppermute | solution.py:34

commit v4 on v3

--- a/solution.py
+++ b/solution.py
@@ -86,7 +86,7 @@
     frames, rows, width = out_ref.shape
     chans = volt_ref.shape[1] // frames
     halo = taps - 1
-    step = 8
+    step = 16
 
     def frame_of(f):
         at = f * chans if isinstance(f, int) else pl.multiple_of(f * chans, chans)

time: 97.3 us -> 97.3 us (level)
  no operation moved by 1% of the time
where the time goes in v4:
time: 97.3 us; the launch traced here: 96.9 us
  blocking collectives  42.4 us (44%)
  starting transfers between devices  29.3 us (30%)
  waiting for transfers between devices  14.1 us (14%)
  Pallas kernels  10 us (10%)
    all_to_all x1, blocking collectives, body(): lax.all_to_all(local, 'inp', split_axis=0, concat_axis=0, tiled=True)  42.4 us
    ppermute x8, starting transfers between devices, tm_shift(): return lax.ppermute(value, 'tm', pairs)  24.6 us
    ppermute x8, waiting for transfers between devices, tm_shift(): return lax.ppermute(value, 'tm', pairs)  12 us
    ppermute x1, starting transfers between devices, from_behind(): return lax.ppermute(value, ('tm', 'freq'), pairs)  4.67 us
    pallas_call x1, Pallas kernels, vis_more(): pl.pallas_call(functools.partial(more_kernel, 2), out_shape=jax.ShapeDtyp...  2.42 us
    ppermute x1, waiting for transfers between devices, from_behind(): return lax.ppermute(value, ('tm', 'freq'), pairs)  2.11 us
  transfers between devices with their start and end apart: 9, of which 7 were waited for; matrix products, arithmetic and copies ran while one was open for 0% of the time, Pallas kernels for 7%

profile of v4, /device:TPU:24, one launch (start us, length us, event | category | flops | bytes accessed | tf_op | source)
XLA Modules:
  0.0 96.9 jit_solution(3719085021497189526)
XLA Ops:
  0.7 1.6 %load.1 = (bf16[2,192,128]{2,1,0:T(8,128)(2,1)S(1)}, bf16[2,4096,128]{2,1,0:T(8,128)(2,1)S(1)}) custom-call(bf16[2,4096,128]{2,1,0:T(8,128)(2,1)} %volt_ref.1), custom_call_target="tpu_custom_call" | custom-call | bytes 4194304 | tf_op jit(solution)/shard_map/load/pallas_call | solution.py:70
  2.3 4.7 %collective-permute-start = (bf16[2,192,128]{2,1,0:T(8,128)(2,1)S(1)}, bf16[2,192,128]{2,1,0:T(8,128)(2,1)S(1)}, u32[]{:S(2)}, u32[]{:S(2)}) collective-permute-start(bf16[2,192,128]{2,1,0:T(8,128)(2,1)S(1)} %get-tuple-element.13), channel_id=1, source_target_pairs={{2,4},{3,5},{0,6},{1,7},{6,8},{7,9},{4,10},{5,11},{10,12},{11,13},... | collective-permute-start | bytes 294920 | tf_op jit(solution)/shard_map/ppermute | solution.py:26
  7.0 1.8 %channelize.1 = (bf16[64,32,128]{2,1,0:T(8,128)(2,1)S(1)}, f32[3,32,128]{2,1,0:T(8,128)S(1)}, bf16[256,128]{1,0:T(8,128)(2,1)S(1)}) custom-call(s32[1]{0:T(128)} %bitcast._, f32[4,32,128]{2,1,0:T(8,128)S(1)} %copy-done, f32[4,64]{1,0:T(4,128)S(1)} %copy-done.1, bf16[2,4096,128]{2,1,0:T(8,128)(2,1)S(1)} %get-tuple-element.11.volt_ref), custom_call_target="tpu_custom_call" | custom-call | flops 536870912 | bytes 3145728 | tf_op jit(solution)/shard_map/channelize/pallas_call | solution.py:146
  8.8 2.1 %collective-permute-done.prior_ref = bf16[2,192,128]{2,1,0:T(8,128)(2,1)S(1)} collective-permute-done((bf16[2,192,128]{2,1,0:T(8,128)(2,1)S(1)}, bf16[2,192,128]{2,1,0:T(8,128)(2,1)S(1)}, u32[]{:S(2)}, u32[]{:S(2)}) %collective-permute-start) | collective-permute-done | bytes 98336 | tf_op jit(solution)/shard_map/ppermute | solution.py:26
  11.1 0.2 copy.17
  11.3 42.4 %all_to_all.5.block_ref.refs_0_ = bf16[16,2,64,128]{3,2,1,0:T(8,128)(2,1)S(1)} all-to-all(bf16[16,2,64,128]{3,2,1,0:T(8,128)(2,1)S(1)} %bitcast.14), channel_id=1, replica_groups=mesh['inp'=16,'tm'=8,'freq'=4] {'inp'}, dimensions={0} | all-to-all | bytes 1048576 | tf_op jit(solution)/shard_map/all_to_all | solution.py:393
  53.7 2.6 %collective-permute-start.1 = (bf16[16,2,64,128]{3,2,1,0:T(8,128)(2,1)S(1)}, bf16[16,2,64,128]{3,2,1,0:T(8,128)(2,1)S(1)}, u32[]{:S(2)}, u32[]{:S(2)}) collective-permute-start(bf16[16,2,64,128]{3,2,1,0:T(8,128)(2,1)S(1)} %all_to_all.5.block_ref.refs_0_), channel_id=1, source_target_pairs={{0,24},{4,28},{8,0},{12,4},{16,8},{20,12},{24,16},{28,20},{1,25},{... | collective-permute-start | bytes 1572872 | tf_op jit(solution)/shard_map/ppermute | solution.py:34
  56.4 2.8 %collective-permute-start.2 = (bf16[16,2,64,128]{3,2,1,0:T(8,128)(2,1)S(1)}, bf16[16,2,64,128]{3,2,1,0:T(8,128)(2,1)S(1)}, u32[]{:S(2)}, u32[]{:S(2)}) collective-permute-start(bf16[16,2,64,128]{3,2,1,0:T(8,128)(2,1)S(1)} %all_to_all.5.block_ref.refs_0_), channel_id=1, source_target_pairs={{0,4},{4,0},{8,12},{12,8},{16,20},{20,16},{24,28},{28,24},{1,5},{5... | collective-permute-start | bytes 1572872 | tf_op jit(solution)/shard_map/ppermute | solution.py:34
  59.2 4.4 %collective-permute-start.3 = (bf16[16,2,64,128]{3,2,1,0:T(8,128)(2,1)S(1)}, bf16[16,2,64,128]{3,2,1,0:T(8,128)(2,1)S(1)}, u32[]{:S(2)}, u32[]{:S(2)}) collective-permute-start(bf16[16,2,64,128]{3,2,1,0:T(8,128)(2,1)S(1)} %all_to_all.5.block_ref.refs_0_), channel_id=1, source_target_pairs={{0,8},{4,12},{8,16},{12,20},{16,24},{20,28},{24,0},{28,4},{1,9},{5... | collective-permute-start | bytes 1572872 | tf_op jit(solution)/shard_map/ppermute | solution.py:34
  63.6 0.9 spectra_out.1
  64.5 3.8 %collective-permute-done.1.refs_0_ = bf16[16,2,64,128]{3,2,1,0:T(8,128)(2,1)S(1)} collective-permute-done((bf16[16,2,64,128]{3,2,1,0:T(8,128)(2,1)S(1)}, bf16[16,2,64,128]{3,2,1,0:T(8,128)(2,1)S(1)}, u32[]{:S(2)}, u32[]{:S(2)}) %collective-permute-start.1) | collective-permute-done | bytes 524320 | tf_op jit(solution)/shard_map/ppermute | solution.py:34
  68.3 1.9 %collective-permute-start.4 = (bf16[16,2,64,128]{3,2,1,0:T(8,128)(2,1)S(1)}, bf16[16,2,64,128]{3,2,1,0:T(8,128)(2,1)S(1)}, u32[]{:S(2)}, u32[]{:S(2)}) collective-permute-start(bf16[16,2,64,128]{3,2,1,0:T(8,128)(2,1)S(1)} %after.3.refs_1_), channel_id=1, source_target_pairs={{0,24},{4,28},{8,0},{12,4},{16,8},{20,12},{24,16},{28,20},{1,25},{... | collective-permute-start | bytes 1572872 | tf_op jit(solution)/shard_map/ppermute | solution.py:34
  70.2 2.2 %collective-permute-start.5 = (bf16[16,2,64,128]{3,2,1,0:T(8,128)(2,1)S(1)}, bf16[16,2,64,128]{3,2,1,0:T(8,128)(2,1)S(1)}, u32[]{:S(2)}, u32[]{:S(2)}) collective-permute-start(bf16[16,2,64,128]{3,2,1,0:T(8,128)(2,1)S(1)} %after.3.refs_1_), channel_id=1, source_target_pairs={{0,4},{4,0},{8,12},{12,8},{16,20},{20,16},{24,28},{28,24},{1,5},{5... | collective-permute-start | bytes 1572872 | tf_op jit(solution)/shard_map/ppermute | solution.py:34
  72.5 0.5 collective-permute-done.3.refs_1_
  73.0 5.2 %collective-permute-start.6 = (bf16[16,2,64,128]{3,2,1,0:T(8,128)(2,1)S(1)}, bf16[16,2,64,128]{3,2,1,0:T(8,128)(2,1)}, u32[]{:S(2)}, u32[]{:S(2)}) collective-permute-start(bf16[16,2,64,128]{3,2,1,0:T(8,128)(2,1)S(1)} %get-tuple-element.18.refs_2_), channel_id=1, source_target_pairs={{0,8},{4,12},{8,16},{12,20},{16,24},{20,28},{24,0},{28,4},{1,9},{5... | collective-permute-start | bytes 1572872 | tf_op jit(solution)/shard_map/ppermute | solution.py:34
  78.2 1.3 %vis_first.1.refs_1_.before_ref = f32[512,2048]{1,0:T(8,128)S(1)} custom-call(s32[1]{0:T(128)} %bitcast.5.own_ref, bf16[16,2,64,128]{3,2,1,0:T(8,128)(2,1)S(1)} %all_to_all.5.block_ref.refs_0_, bf16[16,2,64,128]{3,2,1,0:T(8,128)(2,1)S(1)} %after.3.refs_1_, bf16[16,2,64,128]{3,2,1,0:T(8,128)(2,1)S(1)} %get-tuple-element.18.refs_2_, ...), custom_call_target="tpu_custom_call" | custom-call | flops 1073741824 | bytes 4194304 | tf_op jit(solution)/shard_map/vis_first/pallas_call | solution.py:291
  79.5 1.6 %collective-permute-done.4.refs_0_ = bf16[16,2,64,128]{3,2,1,0:T(8,128)(2,1)S(1)} collective-permute-done((bf16[16,2,64,128]{3,2,1,0:T(8,128)(2,1)S(1)}, bf16[16,2,64,128]{3,2,1,0:T(8,128)(2,1)S(1)}, u32[]{:S(2)}, u32[]{:S(2)}) %collective-permute-start.4) | collective-permute-done | bytes 524320 | tf_op jit(solution)/shard_map/ppermute | solution.py:34
  81.0 3.5 %collective-permute-start.7 = (bf16[8,2,64,128]{3,2,1,0:T(8,128)(2,1)S(1)}, bf16[8,2,64,128]{3,2,1,0:T(8,128)(2,1)S(1)}, u32[]{:S(2)}, u32[]{:S(2)}) collective-permute-start(bf16[8,2,64,128]{3,2,1,0:T(8,128)(2,1)S(1)} %slice.8), channel_id=1, source_target_pairs={{0,4},{4,0},{8,12},{12,8},{16,20},{20,16},{24,28},{28,24},{1,5},{5... | collective-permute-start | bytes 786440 | tf_op jit(solution)/shard_map/ppermute | solution.py:34
  84.5 1.1 %collective-permute-done.5.refs_1_ = bf16[16,2,64,128]{3,2,1,0:T(8,128)(2,1)S(1)} collective-permute-done((bf16[16,2,64,128]{3,2,1,0:T(8,128)(2,1)S(1)}, bf16[16,2,64,128]{3,2,1,0:T(8,128)(2,1)S(1)}, u32[]{:S(2)}, u32[]{:S(2)}) %collective-permute-start.5) | collective-permute-done | bytes 524320 | tf_op jit(solution)/shard_map/ppermute | solution.py:34
  85.6 2.0 %collective-permute-start.8 = (bf16[8,2,64,128]{3,2,1,0:T(8,128)(2,1)S(1)}, bf16[8,2,64,128]{3,2,1,0:T(8,128)(2,1)S(1)}, u32[]{:S(2)}, u32[]{:S(2)}) collective-permute-start(bf16[8,2,64,128]{3,2,1,0:T(8,128)(2,1)S(1)} %slice.9), channel_id=1, source_target_pairs={{0,24},{4,28},{8,0},{12,4},{16,8},{20,12},{24,16},{28,20},{1,25},{... | collective-permute-start | bytes 786440 | tf_op jit(solution)/shard_map/ppermute | solution.py:34
  87.7 2.4 %vis_more.1.total_ref = f32[512,2048]{1,0:T(8,128)S(1)} custom-call(s32[1]{0:T(128)} %bitcast.5.own_ref, f32[512,2048]{1,0:T(8,128)S(1)} %vis_first.1.refs_1_.before_ref, bf16[16,2,64,128]{3,2,1,0:T(8,128)(2,1)S(1)} %after.5.refs_0_, bf16[16,2,64,128]{3,2,1,0:T(8,128)(2,1)S(1)} %collective-permute-done.5.refs_1_, ...), custom_call_target="tpu_custom_call", output_to_operand_aliasing={{}: (1, {})} | custom-call | flops 805306368 | bytes 4194304 | tf_op jit(solution)/shard_map/vis_more/pallas_call | solution.py:309
  90.1 0.7 collective-permute-done.7.low_ref
  90.8 4.3 %collective-permute-done.8.high_ref = bf16[8,2,64,128]{3,2,1,0:T(8,128)(2,1)S(1)} collective-permute-done((bf16[8,2,64,128]{3,2,1,0:T(8,128)(2,1)S(1)}, bf16[8,2,64,128]{3,2,1,0:T(8,128)(2,1)S(1)}, u32[]{:S(2)}, u32[]{:S(2)}) %collective-permute-start.8) | collective-permute-done | bytes 262176 | tf_op jit(solution)/shard_map/ppermute | solution.py:34
  95.1 1.8 %vis_last.1 = bf16[2,256,2048]{2,1,0:T(8,128)(2,1)} custom-call(s32[1]{0:T(128)} %bitcast.5.own_ref, f32[512,2048]{1,0:T(8,128)S(1)} %vis_more.1.total_ref, bf16[8,2,64,128]{3,2,1,0:T(8,128)(2,1)S(1)} %collective-permute-done.7.low_ref, bf16[8,2,64,128]{3,2,1,0:T(8,128)(2,1)S(1)} %collective-permute-done.8.high_ref), custom_call_target="tpu_custom_call" | custom-call | flops 268435456 | bytes 4194304 | tf_op jit(solution)/shard_map/vis_last/pallas_call | solution.py:329
  (12 shorter events, 0.3 us)
Async XLA Ops:
  0.6 6.4 %copy-start = (f32[4,32,128]{2,1,0:T(8,128)S(1)}, f32[4,32,128]{2,1,0:T(8,128)}, u32[]{:S(2)}) copy-start(f32[4,32,128]{2,1,0:T(8,128)} %constant.11.clone.table_ref) | copy-start | bytes 196612
  0.6 6.3 %copy-start.1 = (f32[4,64]{1,0:T(4,128)S(1)}, f32[4,64]{1,0:T(4,128)}, u32[]{:S(2)}) copy-start(f32[4,64]{1,0:T(4,128)} %window_ref.1) | copy-start | bytes 3076
  2.3 8.6 %collective-permute-start = (bf16[2,192,128]{2,1,0:T(8,128)(2,1)S(1)}, bf16[2,192,128]{2,1,0:T(8,128)(2,1)S(1)}, u32[]{:S(2)}, u32[]{:S(2)}) collective-permute-start(bf16[2,192,128]{2,1,0:T(8,128)(2,1)S(1)} %get-tuple-element.13), channel_id=1, source_target_pairs={{2,4},{3,5},{0,6},{1,7},{6,8},{7,9},{4,10},{5,11},{10,12},{11,13},... | collective-permute-start | bytes 294920 | tf_op jit(solution)/shard_map/ppermute | solution.py:26
  53.7 14.6 %collective-permute-start.1 = (bf16[16,2,64,128]{3,2,1,0:T(8,128)(2,1)S(1)}, bf16[16,2,64,128]{3,2,1,0:T(8,128)(2,1)S(1)}, u32[]{:S(2)}, u32[]{:S(2)}) collective-permute-start(bf16[16,2,64,128]{3,2,1,0:T(8,128)(2,1)S(1)} %all_to_all.5.block_ref.refs_0_), channel_id=1, source_target_pairs={{0,24},{4,28},{8,0},{12,4},{16,8},{20,12},{24,16},{28,20},{1,25},{... | collective-permute-start | bytes 1572872 | tf_op jit(solution)/shard_map/ppermute | solution.py:34
  56.4 16.1 %collective-permute-start.2 = (bf16[16,2,64,128]{3,2,1,0:T(8,128)(2,1)S(1)}, bf16[16,2,64,128]{3,2,1,0:T(8,128)(2,1)S(1)}, u32[]{:S(2)}, u32[]{:S(2)}) collective-permute-start(bf16[16,2,64,128]{3,2,1,0:T(8,128)(2,1)S(1)} %all_to_all.5.block_ref.refs_0_), channel_id=1, source_target_pairs={{0,4},{4,0},{8,12},{12,8},{16,20},{20,16},{24,28},{28,24},{1,5},{5... | collective-permute-start | bytes 1572872 | tf_op jit(solution)/shard_map/ppermute | solution.py:34
  59.2 13.8 %collective-permute-start.3 = (bf16[16,2,64,128]{3,2,1,0:T(8,128)(2,1)S(1)}, bf16[16,2,64,128]{3,2,1,0:T(8,128)(2,1)S(1)}, u32[]{:S(2)}, u32[]{:S(2)}) collective-permute-start(bf16[16,2,64,128]{3,2,1,0:T(8,128)(2,1)S(1)} %all_to_all.5.block_ref.refs_0_), channel_id=1, source_target_pairs={{0,8},{4,12},{8,16},{12,20},{16,24},{20,28},{24,0},{28,4},{1,9},{5... | collective-permute-start | bytes 1572872 | tf_op jit(solution)/shard_map/ppermute | solution.py:34
  68.3 12.7 %collective-permute-start.4 = (bf16[16,2,64,128]{3,2,1,0:T(8,128)(2,1)S(1)}, bf16[16,2,64,128]{3,2,1,0:T(8,128)(2,1)S(1)}, u32[]{:S(2)}, u32[]{:S(2)}) collective-permute-start(bf16[16,2,64,128]{3,2,1,0:T(8,128)(2,1)S(1)} %after.3.refs_1_), channel_id=1, source_target_pairs={{0,24},{4,28},{8,0},{12,4},{16,8},{20,12},{24,16},{28,20},{1,25},{... | collective-permute-start | bytes 1572872 | tf_op jit(solution)/shard_map/ppermute | solution.py:34
  70.2 15.4 %collective-permute-start.5 = (bf16[16,2,64,128]{3,2,1,0:T(8,128)(2,1)S(1)}, bf16[16,2,64,128]{3,2,1,0:T(8,128)(2,1)S(1)}, u32[]{:S(2)}, u32[]{:S(2)}) collective-permute-start(bf16[16,2,64,128]{3,2,1,0:T(8,128)(2,1)S(1)} %after.3.refs_1_), channel_id=1, source_target_pairs={{0,4},{4,0},{8,12},{12,8},{16,20},{20,16},{24,28},{28,24},{1,5},{5... | collective-permute-start | bytes 1572872 | tf_op jit(solution)/shard_map/ppermute | solution.py:34
  73.0 14.7 %collective-permute-start.6 = (bf16[16,2,64,128]{3,2,1,0:T(8,128)(2,1)S(1)}, bf16[16,2,64,128]{3,2,1,0:T(8,128)(2,1)}, u32[]{:S(2)}, u32[]{:S(2)}) collective-permute-start(bf16[16,2,64,128]{3,2,1,0:T(8,128)(2,1)S(1)} %get-tuple-element.18.refs_2_), channel_id=1, source_target_pairs={{0,8},{4,12},{8,16},{12,20},{16,24},{20,28},{24,0},{28,4},{1,9},{5... | collective-permute-start | bytes 1572872 | tf_op jit(solution)/shard_map/ppermute | solution.py:34
  81.0 9.8 %collective-permute-start.7 = (bf16[8,2,64,128]{3,2,1,0:T(8,128)(2,1)S(1)}, bf16[8,2,64,128]{3,2,1,0:T(8,128)(2,1)S(1)}, u32[]{:S(2)}, u32[]{:S(2)}) collective-permute-start(bf16[8,2,64,128]{3,2,1,0:T(8,128)(2,1)S(1)} %slice.8), channel_id=1, source_target_pairs={{0,4},{4,0},{8,12},{12,8},{16,20},{20,16},{24,28},{28,24},{1,5},{5... | collective-permute-start | bytes 786440 | tf_op jit(solution)/shard_map/ppermute | solution.py:34
  85.6 9.5 %collective-permute-start.8 = (bf16[8,2,64,128]{3,2,1,0:T(8,128)(2,1)S(1)}, bf16[8,2,64,128]{3,2,1,0:T(8,128)(2,1)S(1)}, u32[]{:S(2)}, u32[]{:S(2)}) collective-permute-start(bf16[8,2,64,128]{3,2,1,0:T(8,128)(2,1)S(1)} %slice.9), channel_id=1, source_target_pairs={{0,24},{4,28},{8,0},{12,4},{16,8},{20,12},{24,16},{28,20},{1,25},{... | collective-permute-start | bytes 786440 | tf_op jit(solution)/shard_map/ppermute | solution.py:34
